TPU v7x, 128 devices: a whole 4x4x4 slice. The times are simulated.
128 devices in a mesh: batch: 32 (over z, x_lo, y), tensor: 4 (over x_hi, core).
Axes of the slice: x: 4 (x_hi: 2, x_lo: 2; x = x_hi * 2 + x_lo), y: 4, z: 4, core: 2. Of those that a mesh axis runs over, the one named last changes fastest.
Arguments:
- target_latents: bfloat16 [8192, 2048], P('batch', 'tensor'), may hold values from -6 to 6
- walk_noise: bfloat16 [4, 8192, 2048], P(None, 'batch', 'tensor'), may hold values from -6 to 6
- step_sizes: float32 [4], replicated, may hold values from 0.05 to 0.2
- back_gain: float32 [2048], replicated, may hold values from 0.1 to 1.9
- back_expand: bfloat16 [2048, 4096], P(None, 'tensor'), may hold values from -0.125 to 0.125
- back_clock: float32 [4096], P('tensor'), may hold values from -4 to 4
- back_reduce: bfloat16 [4096, 2048], P('tensor'), may hold values from -0.09375 to 0.09375
- bridge_times: float32 [8192], P('batch'), may hold values from 0.05 to 0.9
- bridge_noise: bfloat16 [8192, 2048], P('batch', 'tensor'), may hold values from -6 to 6
- fore_gain: float32 [2048], replicated, may hold values from 0.1 to 1.9
- fore_expand: bfloat16 [2048, 4096], P(None, 'tensor'), may hold values from -0.125 to 0.125
- fore_clock: float32 [4096], P('tensor'), may hold values from -4 to 4
- fore_reduce: bfloat16 [4096, 2048], P('tensor'), may hold values from -0.09375 to 0.09375
Outputs:
- walk_end: float32 [8192, 2048], P('batch', 'tensor')
- grad_expand: float32 [2048, 4096], P('batch', 'tensor')
- grad_reduce_t: float32 [2048, 4096], P('batch', 'tensor')
All inputs are finite; a program needn't handle non-finite values.
Results may differ from a plain program's by a relative error of at most 0.0055.
Values may be sent and summed in bfloat16 or wider, within the bound.
A program may use at most 128 MiB of HBM per device.

v0:
```python
import jax
import jax.numpy as jnp
from jax import lax
from jax.sharding import PartitionSpec as P

NOISE_LEVEL = 0.5
EPSILON = 1e-06


def normalize(rows, gain):
    float_rows = rows.astype(jnp.float32)
    factor = lax.rsqrt(jnp.mean(float_rows * float_rows, axis=1, keepdims=True) + EPSILON)
    return (float_rows * factor * gain).astype(jnp.bfloat16)


def body(
    target_latents,
    walk_noise,
    step_sizes,
    back_gain,
    back_expand,
    back_clock,
    back_reduce,
    bridge_times,
    bridge_noise,
    fore_gain,
    fore_expand,
    fore_clock,
    fore_reduce,
):
    walk_state = target_latents.astype(jnp.float32)
    walk_clock = jnp.float32(1.0)
    for step_index in range(walk_noise.shape[0]):
        full_rows = lax.all_gather(walk_state.astype(jnp.bfloat16), "tensor", axis=1, tiled=True)
        normed = normalize(full_rows, back_gain)
        hidden = (
            jnp.dot(normed, back_expand, preferred_element_type=jnp.float32)
            + walk_clock * back_clock
        )
        active = jax.nn.silu(hidden).astype(jnp.bfloat16)
        partial_drift = jnp.dot(active, back_reduce, preferred_element_type=jnp.float32)
        drift = lax.psum_scatter(partial_drift, "tensor", scatter_dimension=1, tiled=True)
        step_width = step_sizes[step_index]
        walk_state = (
            walk_state
            - step_width * drift
            + jnp.sqrt(step_width) * NOISE_LEVEL * walk_noise[step_index].astype(jnp.float32)
        )
        walk_clock = walk_clock - step_width
    walk_short = walk_state.astype(jnp.bfloat16)
    start_rows, end_rows = (
        lax.all_to_all(walk_short, "batch", split_axis=0, concat_axis=0, tiled=True),
        lax.all_to_all(target_latents, "batch", split_axis=0, concat_axis=0, tiled=True),
    )
    row_times, row_noise = (bridge_times, bridge_noise)
    start_float = start_rows.astype(jnp.float32)
    end_float = end_rows.astype(jnp.float32)
    bridge_tau = row_times[:, None]
    interpolant = (
        (1.0 - bridge_tau) * start_float
        + bridge_tau * end_float
        + jnp.sqrt(bridge_tau * (1.0 - bridge_tau)) * NOISE_LEVEL * row_noise.astype(jnp.float32)
    )
    target_flow = (end_float - interpolant) / (1.0 - bridge_tau)
    full_rows = lax.all_gather(interpolant.astype(jnp.bfloat16), "tensor", axis=1, tiled=True)
    normed = normalize(full_rows, fore_gain)
    hidden = (
        jnp.dot(normed, fore_expand, preferred_element_type=jnp.float32) + bridge_tau * fore_clock
    )
    active = jax.nn.silu(hidden).astype(jnp.bfloat16)
    partial_guess = jnp.dot(active, fore_reduce, preferred_element_type=jnp.float32)
    predicted = lax.psum_scatter(partial_guess, "tensor", scatter_dimension=1, tiled=True)
    total_rows = row_times.shape[0] * lax.axis_size("batch")
    loss_scale = 1.0 / jnp.sqrt(jnp.float32(total_rows))
    scaled_error = ((predicted - target_flow) * loss_scale).astype(jnp.bfloat16)
    full_error = lax.all_gather(scaled_error, "tensor", axis=1, tiled=True)
    back_hidden = lax.dot_general(
        full_error, fore_reduce, (((1,), (1,)), ((), ())), preferred_element_type=jnp.float32
    )
    sigmoid_part = jax.nn.sigmoid(hidden)
    silu_slope = sigmoid_part * (1.0 + hidden * (1.0 - sigmoid_part))
    hidden_grad = (back_hidden * silu_slope).astype(jnp.bfloat16)
    local_width = hidden_grad.shape[1]
    grad_first = lax.dot_general(
        normed, hidden_grad, (((0,), (0,)), ((), ())), preferred_element_type=jnp.float32
    )
    grad_second = lax.dot_general(
        full_error, active, (((0,), (0,)), ((), ())), preferred_element_type=jnp.float32
    )
    summed = lax.psum_scatter(
        jnp.concatenate([grad_first, grad_second], axis=1), "batch", scatter_dimension=0, tiled=True
    )
    grad_expand = summed[:, :local_width]
    grad_reduce_t = summed[:, local_width:]
    return (walk_state, grad_expand, grad_reduce_t)


def solution(mesh):
    placed = (
        P("batch", "tensor"),
        P(None, "batch", "tensor"),
        P(),
        P(),
        P(None, "tensor"),
        P("tensor"),
        P("tensor", None),
        P("batch"),
        P("batch", "tensor"),
        P(),
        P(None, "tensor"),
        P("tensor"),
        P("tensor", None),
    )
    return jax.shard_map(
        body,
        mesh=mesh,
        in_specs=placed,
        out_specs=(P("batch", "tensor"), P("batch", "tensor"), P("batch", "tensor")),
        check_vma=False,
    )
```

profile of v0, /device:TPU:0, one launch (start us, length us, event | category | flops | bytes accessed | tf_op | source)
XLA Modules:
  0.0 645.5 jit_solution(969695153629023347)
XLA Ops:
  7.2 0.0 all-gather.7.cloned.1.call-start
  7.2 0.7 all-gather.7.cloned.1.call-update
  7.9 0.0 reduce-scatter.9.cloned.1.call-start
  7.9 25.0 %all-gather.7.cloned.1.call-done = bf16[256,2048]{1,0:T(8,128)(2,1)} async-done(((bf16[256,512]{1,0:T(8,128)(2,1)}), bf16[256,2048]{1,0:T(8,128)(2,1)}) %all-gather.7.cloned.1.call-update) | async-done | bytes 1048592 | tf_op jit(solution)/shard_map/all_gather | solution.py:34
  32.9 1.5 fusion
  34.4 0.0 copy-start.10
  34.5 7.7 %fusion.42 = f32[256,2048]{1,0:T(8,128)} fusion(bf16[1024,2048]{1,0:T(8,128)(2,1)} %param.19, bf16[2048,1024]{1,0:T(8,128)(2,1)} %param.17, bf16[256,2048]{1,0:T(8,128)(2,1)} %all-gather.7.cloned.1.call-done, f32[2048]{0:T(1024)} %param.16, f32[256]{0:T(256)S(1)} %add_rsqrt_fusion.4, f32[1024]{0:T(1024)} %param.18), kind=kOutput, calls=%fused_computation.52 | convolution fusion | flops 2151153664 | bytes 11547648 | tf_op jit(solution)/shard_map/dot_general | solution.py:41
  42.1 0.0 reduce-scatter.9.cloned.1.call-update
  42.2 0.0 all-gather.9.cloned.1.call-start
  42.2 0.7 fusion.82
  43.6 36.5 %reduce-scatter.9.cloned.1.call-done = f32[256,512]{1,0:T(8,128)} async-done(((f32[256,2048]{1,0:T(8,128)}), f32[256,512]{1,0:T(8,128)}) %reduce-scatter.9.cloned.1.call-update) | async-done | bytes 524304 | tf_op jit(solution)/shard_map/reduce_scatter | solution.py:42
  80.1 2.6 fusion.71
  82.7 0.0 all-gather.9.cloned.1.call-update
  82.7 0.0 reduce-scatter.11.cloned.1.call-start
  84.7 18.3 %all-gather.9.cloned.1.call-done = bf16[256,2048]{1,0:T(8,128)(2,1)} async-done(((bf16[256,512]{1,0:T(8,128)(2,1)}), bf16[256,2048]{1,0:T(8,128)(2,1)}) %all-gather.9.cloned.1.call-update) | async-done | bytes 1048592 | tf_op jit(solution)/shard_map/all_gather | solution.py:34
  103.0 1.5 fusion.3
  104.6 7.6 %fusion.45 = f32[256,2048]{1,0:T(8,128)} fusion(bf16[1024,2048]{1,0:T(8,128)(2,1)} %param.19, bf16[2048,1024]{1,0:T(8,128)(2,1)} %param.17, bf16[256,2048]{1,0:T(8,128)(2,1)} %all-gather.9.cloned.1.call-done, f32[256]{0:T(256)S(1)} %add_rsqrt_fusion.3, f32[2048]{0:T(1024)S(1)} %copy-done.12, f32[1024]{0:T(1024)S(1)} %get-tuple-element.16), kind=kOutput, calls=%fused_computation.53 | convolution fusion | flops 2151153664 | bytes 11547648 | tf_op jit(solution)/shard_map/dot_general | solution.py:41
  112.2 0.0 reduce-scatter.11.cloned.1.call-update
  112.2 0.0 all-gather.11.cloned.1.call-start
  113.0 37.2 %reduce-scatter.11.cloned.1.call-done = f32[256,512]{1,0:T(8,128)} async-done(((f32[256,2048]{1,0:T(8,128)}), f32[256,512]{1,0:T(8,128)}) %reduce-scatter.11.cloned.1.call-update) | async-done | bytes 524304 | tf_op jit(solution)/shard_map/reduce_scatter | solution.py:42
  150.2 3.3 fusion.80
  153.5 0.0 all-gather.11.cloned.1.call-update
  153.5 0.0 reduce-scatter.13.cloned.1.call-start
  153.5 20.3 %all-gather.11.cloned.1.call-done = bf16[256,2048]{1,0:T(8,128)(2,1)} async-done(((bf16[256,512]{1,0:T(8,128)(2,1)}), bf16[256,2048]{1,0:T(8,128)(2,1)}) %all-gather.11.cloned.1.call-update) | async-done | bytes 1048592 | tf_op jit(solution)/shard_map/all_gather | solution.py:34
  173.8 1.5 fusion.6
  175.4 7.6 %fusion.48 = f32[256,2048]{1,0:T(8,128)} fusion(bf16[1024,2048]{1,0:T(8,128)(2,1)} %param.19, bf16[2048,1024]{1,0:T(8,128)(2,1)} %param.17, bf16[256,2048]{1,0:T(8,128)(2,1)} %all-gather.11.cloned.1.call-done, f32[256]{0:T(256)S(1)} %add_rsqrt_fusion.2, f32[2048]{0:T(1024)S(1)} %copy-done.12, f32[1024]{0:T(1024)S(1)} %get-tuple-element.17), kind=kOutput, calls=%fused_computation.54 | convolution fusion | flops 2151153664 | bytes 11547648 | tf_op jit(solution)/shard_map/dot_general | solution.py:41
  183.0 0.0 reduce-scatter.13.cloned.1.call-update
  183.0 0.0 all-gather.13.cloned.1.call-start
  183.8 37.2 %reduce-scatter.13.cloned.1.call-done = f32[256,512]{1,0:T(8,128)} async-done(((f32[256,2048]{1,0:T(8,128)}), f32[256,512]{1,0:T(8,128)}) %reduce-scatter.13.cloned.1.call-update) | async-done | bytes 524304 | tf_op jit(solution)/shard_map/reduce_scatter | solution.py:42
  220.9 2.6 fusion.77
  223.5 0.0 all-gather.13.cloned.1.call-update
  223.5 0.0 reduce-scatter.15.cloned.1.call-start
  223.6 20.3 %all-gather.13.cloned.1.call-done = bf16[256,2048]{1,0:T(8,128)(2,1)} async-done(((bf16[256,512]{1,0:T(8,128)(2,1)}), bf16[256,2048]{1,0:T(8,128)(2,1)}) %all-gather.13.cloned.1.call-update) | async-done | bytes 1048592 | tf_op jit(solution)/shard_map/all_gather | solution.py:34
  243.9 1.5 fusion.9
  245.4 7.6 %fusion.51 = f32[256,2048]{1,0:T(8,128)} fusion(bf16[1024,2048]{1,0:T(8,128)(2,1)} %param.19, bf16[2048,1024]{1,0:T(8,128)(2,1)} %param.17, bf16[256,2048]{1,0:T(8,128)(2,1)} %all-gather.13.cloned.1.call-done, f32[256]{0:T(256)S(1)} %add_rsqrt_fusion.1, f32[2048]{0:T(1024)S(1)} %copy-done.12, f32[1024]{0:T(1024)S(1)} %get-tuple-element.15), kind=kOutput, calls=%fused_computation.55 | convolution fusion | flops 2151153664 | bytes 11547648 | tf_op jit(solution)/shard_map/dot_general | solution.py:41
  253.0 0.0 reduce-scatter.15.cloned.1.call-update
  253.1 7.4 %all-to-all-start.1 = ((bf16[32,8,512]{2,1,0:T(8,128)(2,1)}), bf16[32,8,512]{2,1,0:T(8,128)(2,1)S(1)}, u32[]{:S(2)}, u32[]{:S(2)}) async-start(bf16[32,8,512]{2,1,0:T(8,128)(2,1)} %bitcast.10), calls=%async_computation.5 | async-start | bytes 524288 | tf_op jit(solution)/shard_map/all_to_all | solution.py:53
  261.2 29.8 %reduce-scatter.15.cloned.1.call-done = f32[256,512]{1,0:T(8,128)} async-done(((f32[256,2048]{1,0:T(8,128)}), f32[256,512]{1,0:T(8,128)}) %reduce-scatter.15.cloned.1.call-update) | async-done | bytes 524304 | tf_op jit(solution)/shard_map/reduce_scatter | solution.py:42
  291.0 3.5 convert_bitcast_fusion
  294.5 7.3 %all-to-all-start = ((bf16[32,8,512]{2,1,0:T(8,128)(2,1)}), bf16[32,8,512]{2,1,0:T(8,128)(2,1)S(1)}, u32[]{:S(2)}, u32[]{:S(2)}) async-start(bf16[32,8,512]{2,1,0:T(8,128)(2,1)} %get-tuple-element.9), calls=%async_computation.4 | async-start | bytes 524288 | tf_op jit(solution)/shard_map/all_to_all | solution.py:52
  301.7 0.0 all-gather.15.cloned.1.call-start
  301.8 9.1 %all-to-all-done = bf16[32,8,512]{2,1,0:T(8,128)(2,1)S(1)} async-done(((bf16[32,8,512]{2,1,0:T(8,128)(2,1)}), bf16[32,8,512]{2,1,0:T(8,128)(2,1)S(1)}, u32[]{:S(2)}, u32[]{:S(2)}) %all-to-all-start) | async-done | bytes 262176 | tf_op jit(solution)/shard_map/all_to_all | solution.py:52
  310.9 0.9 fusion.68
  311.8 0.0 all-gather.15.cloned.1.call-update
  311.8 0.2 reduce-scatter.17.cloned.1.call-start
  312.1 17.1 %all-gather.15.cloned.1.call-done = bf16[256,2048]{1,0:T(8,128)(2,1)} async-done(((bf16[256,512]{1,0:T(8,128)(2,1)}), bf16[256,2048]{1,0:T(8,128)(2,1)}) %all-gather.15.cloned.1.call-update) | async-done | bytes 1048592 | tf_op jit(solution)/shard_map/all_gather | solution.py:65
  329.2 1.5 fusion.12
  330.7 4.0 convolution_add_fusion
  334.7 2.7 fusion.79
  337.4 0.0 reduce-scatter.17.cloned.1.call-update
  337.4 0.0 all-gather.17.cloned.1.call-start
  337.5 37.9 %reduce-scatter.17.cloned.1.call-done = f32[256,512]{1,0:T(8,128)} async-done(((f32[256,2048]{1,0:T(8,128)}), f32[256,512]{1,0:T(8,128)}) %reduce-scatter.17.cloned.1.call-update) | async-done | bytes 524304 | tf_op jit(solution)/shard_map/reduce_scatter | solution.py:72
  375.4 2.1 fusion.67
  377.4 0.0 all-gather.17.cloned.1.call-update
  377.4 0.0 reduce-scatter.19.cloned.1.call-start
  377.5 20.4 %all-gather.17.cloned.1.call-done = bf16[256,2048]{1,0:T(8,128)(2,1)} async-done(((bf16[256,512]{1,0:T(8,128)(2,1)}), bf16[256,2048]{1,0:T(8,128)(2,1)}) %all-gather.17.cloned.1.call-update) | async-done | bytes 1048592 | tf_op jit(solution)/shard_map/all_gather | solution.py:76
  397.9 8.5 %fusion.16 = f32[2048,1024]{0,1:T(8,128)} fusion(bf16[256,2048]{1,0:T(8,128)(2,1)} %all-gather.17.cloned.1.call-done, bf16[1024,2048]{1,0:T(8,128)(2,1)} %param.25, f32[256,1024]{1,0:T(8,128)S(1)} %convolution_add_fusion, bf16[256,2048]{1,0:T(8,128)(2,1)S(1)} %copy-done.3, f32[2048]{0:T(1024)S(1)} %copy-done.9, f32[256]{0:T(256)S(1)} %add_rsqrt_fusion), kind=kOutput, calls=%fused_computation.33 | convolution fusion | flops 2151940096 | bytes 15737856 | tf_op jit(solution)/shard_map/dot_general | solution.py:84
  406.4 1.4 fusion.78
  407.8 2.0 copy-done
  409.8 6.3 pad_maximum_fusion
  416.1 17.6 %copy.20 = f32[2048,2048]{1,0:T(8,128)} copy(f32[2048,2048]{0,1:T(8,128)} %pad_maximum_fusion) | data formatting | bytes 33554432
  433.7 0.0 reduce-scatter.19.cloned.1.call-update
  433.7 203.0 %reduce-scatter.19.cloned.1.call-done = f32[64,2048]{1,0:T(8,128)} async-done(((f32[2048,2048]{1,0:T(8,128)}), f32[64,2048]{1,0:T(8,128)}) %reduce-scatter.19.cloned.1.call-update) | async-done | bytes 524304
  636.7 1.9 fusion.81
  (34 shorter events, 0.1 us)
Async XLA Ops:
  7.2 25.7 %all-gather.7.cloned.1.call-start = ((), (), s32[]{:S(2)}) async-start(), calls=%async_computation.8 | async-start | bytes 1310720 | tf_op jit(solution)/shard_map/all_gather | solution.py:34
  7.9 72.2 %reduce-scatter.9.cloned.1.call-start = ((), (), s32[]{:S(2)}) async-start(), calls=%async_computation.9 | async-start | bytes 2621440 | tf_op jit(solution)/shard_map/reduce_scatter | solution.py:42
  34.4 7.8 %copy-start.10 = (f32[4]{0:T(128)S(1)}, f32[4]{0:T(128)}, u32[]{:S(2)}) copy-start(f32[4]{0:T(128)} %param.15) | copy-start | bytes 52
  34.4 45.6 %copy-start.4 = (bf16[4,256,512]{2,1,0:T(8,128)(2,1)S(1)}, bf16[4,256,512]{2,1,0:T(8,128)(2,1)}, u32[]{:S(2)}) copy-start(bf16[4,256,512]{2,1,0:T(8,128)(2,1)} %param.14) | copy-start | bytes 3145732
  34.5 50.3 %copy-start.11 = (f32[1024]{0:T(1024)S(1)}, f32[1024]{0:T(1024)}, u32[]{:S(2)}) copy-start(f32[1024]{0:T(1024)} %param.18) | copy-start | bytes 12292
  42.1 62.4 %copy-start.12 = (f32[2048]{0:T(1024)S(1)}, f32[2048]{0:T(1024)}, u32[]{:S(2)}) copy-start(f32[2048]{0:T(1024)} %param.16) | copy-start | bytes 24580
  42.2 60.9 %all-gather.9.cloned.1.call-start = ((), (), s32[]{:S(2)}) async-start(), calls=%async_computation.10 | async-start | bytes 1310720 | tf_op jit(solution)/shard_map/all_gather | solution.py:34
  82.7 67.5 %reduce-scatter.11.cloned.1.call-start = ((), (), s32[]{:S(2)}) async-start(), calls=%async_computation.11 | async-start | bytes 2621440 | tf_op jit(solution)/shard_map/reduce_scatter | solution.py:42
  104.6 45.6 %copy-start.6 = (f32[256,512]{1,0:T(8,128)S(1)}, f32[256,512]{1,0:T(8,128)}, u32[]{:S(2)}) copy-start(f32[256,512]{1,0:T(8,128)} %reduce-scatter.9.cloned.1.call-done) | copy-start | bytes 1572868
  112.2 61.6 %all-gather.11.cloned.1.call-start = ((), (), s32[]{:S(2)}) async-start(), calls=%async_computation.12 | async-start | bytes 1310720 | tf_op jit(solution)/shard_map/all_gather | solution.py:34
  153.5 67.4 %reduce-scatter.13.cloned.1.call-start = ((), (), s32[]{:S(2)}) async-start(), calls=%async_computation.13 | async-start | bytes 2621440 | tf_op jit(solution)/shard_map/reduce_scatter | solution.py:42
  183.0 60.9 %all-gather.13.cloned.1.call-start = ((), (), s32[]{:S(2)}) async-start(), calls=%async_computation.14 | async-start | bytes 1310720 | tf_op jit(solution)/shard_map/all_gather | solution.py:34
  223.5 67.5 %reduce-scatter.15.cloned.1.call-start = ((), (), s32[]{:S(2)}) async-start(), calls=%async_computation.15 | async-start | bytes 2621440 | tf_op jit(solution)/shard_map/reduce_scatter | solution.py:42
  245.4 45.6 %copy-start.5 = (f32[256,512]{1,0:T(8,128)S(1)}, f32[256,512]{1,0:T(8,128)}, u32[]{:S(2)}) copy-start(f32[256,512]{1,0:T(8,128)} %reduce-scatter.13.cloned.1.call-done) | copy-start | bytes 1572868
  253.0 48.7 %copy-start.8 = (f32[256]{0:T(256)S(1)}, f32[256]{0:T(256)}, u32[]{:S(2)}) copy-start(f32[256]{0:T(256)} %param.20) | copy-start | bytes 3076
  253.0 57.8 %copy-start.7 = (bf16[256,512]{1,0:T(8,128)(2,1)S(1)}, bf16[256,512]{1,0:T(8,128)(2,1)}, u32[]{:S(2)}) copy-start(bf16[256,512]{1,0:T(8,128)(2,1)} %param.21) | copy-start | bytes 786436
  253.0 77.7 %copy-start.9 = (f32[2048]{0:T(1024)S(1)}, f32[2048]{0:T(1024)}, u32[]{:S(2)}) copy-start(f32[2048]{0:T(1024)} %param.22) | copy-start | bytes 24580
  253.0 77.7 %copy-start.13 = (f32[1024]{0:T(1024)S(1)}, f32[1024]{0:T(1024)}, u32[]{:S(2)}) copy-start(f32[1024]{0:T(1024)} %param.24) | copy-start | bytes 12292
  253.1 41.4 %all-to-all-start.1 = ((bf16[32,8,512]{2,1,0:T(8,128)(2,1)}), bf16[32,8,512]{2,1,0:T(8,128)(2,1)S(1)}, u32[]{:S(2)}, u32[]{:S(2)}) async-start(bf16[32,8,512]{2,1,0:T(8,128)(2,1)} %bitcast.10), calls=%async_computation.5 | async-start | bytes 524288 | tf_op jit(solution)/shard_map/all_to_all | solution.py:53
  294.5 16.4 %all-to-all-start = ((bf16[32,8,512]{2,1,0:T(8,128)(2,1)}), bf16[32,8,512]{2,1,0:T(8,128)(2,1)S(1)}, u32[]{:S(2)}, u32[]{:S(2)}) async-start(bf16[32,8,512]{2,1,0:T(8,128)(2,1)} %get-tuple-element.9), calls=%async_computation.4 | async-start | bytes 524288 | tf_op jit(solution)/shard_map/all_to_all | solution.py:52
  301.7 27.5 %all-gather.15.cloned.1.call-start = ((), (), s32[]{:S(2)}) async-start(), calls=%async_computation.16 | async-start | bytes 1310720 | tf_op jit(solution)/shard_map/all_gather | solution.py:65
  311.8 63.5 %reduce-scatter.17.cloned.1.call-start = ((), (), s32[]{:S(2)}) async-start(), calls=%async_computation.17 | async-start | bytes 2621440 | tf_op jit(solution)/shard_map/reduce_scatter | solution.py:72
  330.7 4.0 copy-start.2
  334.7 63.2 %copy-start.3 = (bf16[256,2048]{1,0:T(8,128)(2,1)S(1)}, bf16[256,2048]{1,0:T(8,128)(2,1)}, u32[]{:S(2)}) copy-start(bf16[256,2048]{1,0:T(8,128)(2,1)} %all-gather.15.cloned.1.call-done) | copy-start | bytes 3145732
  337.4 60.5 %all-gather.17.cloned.1.call-start = ((), (), s32[]{:S(2)}) async-start(), calls=%async_computation.18 | async-start | bytes 1310720 | tf_op jit(solution)/shard_map/all_gather | solution.py:76
  377.4 259.3 %reduce-scatter.19.cloned.1.call-start = ((), (), s32[]{:S(2)}) async-start(), calls=%async_computation.19 | async-start | bytes 17301504
  397.9 8.5 %copy-start.1 = (bf16[256,2048]{1,0:T(8,128)(2,1)S(1)}, bf16[256,2048]{1,0:T(8,128)(2,1)}, u32[]{:S(2)}) copy-start(bf16[256,2048]{1,0:T(8,128)(2,1)} %all-gather.17.cloned.1.call-done) | copy-start | bytes 3145732
  406.4 3.4 copy-start
Sparse Core Ops, SparseCore 0:
  9.7 23.1 all-gather.6
  42.3 37.7 reduce-scatter.8
  82.8 20.1 all-gather.8
  112.4 37.7 reduce-scatter.10
  153.6 20.1 all-gather.10
  183.1 37.7 reduce-scatter.12
  223.6 20.1 all-gather.12
  253.2 37.7 reduce-scatter.14
  311.9 17.1 all-gather.14
  337.5 37.7 reduce-scatter.16
  377.7 20.1 all-gather.16
  433.8 202.8 reduce-scatter.18
where the time goes:
time: 647 us; the launch traced here: 645 us
  waiting for transfers between devices  513 us (79%)
  matrix products  47 us (7%)
  other arithmetic  28.8 us (4%)
  local copies, waits for them, and re-layouts  22.2 us (3%)
  between operations  19.2 us (3%)
  starting transfers between devices  15.4 us (2%)
    unnamed x13, waiting for transfers between devices  204 us
    reduce_scatter x4, waiting for transfers between devices, body(): lax.psum_scatter(partial_drift, 'tensor', scatter_dimension=1, tiled=True)  141 us
    all_gather x4, waiting for transfers between devices, body(): lax.all_gather(walk_state.astype(jnp.bfloat16), 'tensor', axis=1, tiled=T...  83.9 us
    reduce_scatter x1, waiting for transfers between devices, body(): lax.psum_scatter(partial_guess, 'tensor', scatter_dimension=1, tiled=True)  37.9 us
    dot_general x4, matrix products, body(): jnp.dot(active, back_reduce, preferred_element_type=jnp.float32)  30.5 us
    all_gather x1, waiting for transfers between devices, body(): full_error = lax.all_gather(scaled_error, 'tensor', axis=1, tiled=True)  20.4 us
    unnamed x29, local copies, waits for them, and re-layouts  19.7 us
    all_gather x1, waiting for transfers between devices, body(): lax.all_gather(interpolant.astype(jnp.bfloat16), 'tensor', axis=1, tiled=...  17.1 us
  transfers between devices with their start and end apart: 14, of which 13 were waited for; matrix products, arithmetic and copies ran while one was open for 1% of the time, Pallas kernels for 0%

commit v1 on v0

v1 whole, which is shorter than its diff:
```python
import jax
import jax.numpy as jnp
from jax import lax
from jax.experimental import pallas as pl
from jax.experimental.pallas import tpu as pltpu
from jax.sharding import PartitionSpec as P

NOISE_LEVEL = 0.5
EPSILON = 1e-06
MESH = pl.DeviceIdType.MESH
F32 = jnp.float32
BF16 = jnp.bfloat16
STREAMS = 2
ROWS = 128


def place():
    b = lax.axis_index("batch")
    t = lax.axis_index("tensor")
    return b // 8, (b // 4) % 2, b % 4, t // 2, t % 2


def device(z, l, y, h, c):
    return (z * 8 + l * 4 + y, h * 2 + c)


def remote(src, dst, send_sem, recv_sem, dev):
    return pltpu.make_async_remote_copy(
        src_ref=src, dst_ref=dst, send_sem=send_sem, recv_sem=recv_sem, device_id=dev, device_id_type=MESH
    )


def greet(devices):
    barrier = pltpu.get_barrier_semaphore()
    for dev in devices:
        pl.semaphore_signal(barrier, inc=1, device_id=dev, device_id_type=MESH)
    return lambda: pl.semaphore_wait(barrier, len(devices))


def batch_peers(z, l, y, h, c):
    peers = [device(z, 1 - l, y, h, c)]
    peers += [device(z, l, (y + d) % 4, h, c) for d in (1, 2, 3)]
    peers += [device((z + d) % 4, l, y, h, c) for d in (1, 2, 3)]
    return peers


def net_kernel(
    x_ref, wn_hbm, steps_ref, bg_ref, be_hbm, bc_ref, br_hbm, bt_ref, bn_ref, fg_ref, fe_hbm, fc_ref, fr_hbm,
    walk_ref, normed_ref, err_ref, hg_ref, act_ref,
    be, br, fe, fr, wn, u, nb, ab, pcs, pcr, pfs, pfr, own, flow, hid, tau, m0, m1, m2, m3,
    load_sem, ss, rs, ms, mr,
):
    z, l, y, h, c = place()
    core_dev = device(z, l, y, h, 1 - c)
    far_dev = device(z, l, y, 1 - h, c)
    q_own, q_far = 2 * h + c, 2 * (1 - h) + c

    loads = [
        pltpu.make_async_copy(src, dst, load_sem.at[i])
        for i, (src, dst) in enumerate(((be_hbm, be), (br_hbm, br), (wn_hbm, wn), (fe_hbm, fe), (fr_hbm, fr)))
    ]
    for load in loads:
        load.start()
    arrived = greet([core_dev, far_dev] + batch_peers(z, l, y, h, c))

    def rows(s):
        return slice(s * ROWS, (s + 1) * ROWS)

    def ag_core(s):
        return remote(u.at[s, q_own], u.at[s, q_own], ss.at[0, s], rs.at[0, s], core_dev)

    def ag_far(s):
        return remote(u.at[s, q_own], u.at[s, q_own], ss.at[1, s], rs.at[1, s], far_dev)

    def ag_fwd(s):
        return remote(u.at[s, q_far], u.at[s, q_far], ss.at[2, s], rs.at[2, s], core_dev)

    def rs_core(s, i):
        side = (1 - h) if i == 0 else h
        return remote(pcs.at[s, side], pcr.at[s, side], ss.at[3 + i, s], rs.at[3 + i, s], core_dev)

    def rs_far(s):
        return remote(pfs.at[s], pfr.at[s], ss.at[5, s], rs.at[5, s], far_dev)

    def gather_start(s):
        ag_far(s).start()
        ag_core(s).start()

    def gather_wait(s):
        ag_far(s).wait_recv()
        ag_fwd(s).start()
        ag_core(s).wait_recv()
        ag_fwd(s).wait_recv()

    def put_own(s, value):
        ag_core(s).wait_send()
        ag_far(s).wait_send()
        u[s, q_own] = value.astype(BF16)

    def normalize(s, gain_ref):
        parts = [u[s, q].astype(F32) for q in range(4)]
        total = sum(jnp.sum(p * p, axis=1, keepdims=True) for p in parts)
        factor = lax.rsqrt(total * (1.0 / 2048.0) + EPSILON)
        for q in range(4):
            nb[:, 512 * q : 512 * (q + 1)] = (parts[q] * factor * gain_ref[:, 512 * q : 512 * (q + 1)]).astype(BF16)

    def reduce_start(s, active, reduce_ref):
        for i in range(2):
            side = (1 - h) if i == 0 else h
            column = pl.multiple_of((2 * side + 1 - c) * 512, 512)
            pcs[s, side] = jnp.dot(active, reduce_ref[:, pl.ds(column, 512)], preferred_element_type=F32)
            rs_core(s, i).start()
        part = jnp.dot(
            active, reduce_ref[:, pl.ds(pl.multiple_of(q_far * 512, 512), 512)], preferred_element_type=F32
        )
        rs_core(s, 0).wait_recv()
        ag_fwd(s).wait_send()
        pfs[s] = (part + pcr[s, 1 - h]).astype(BF16)
        rs_far(s).start()
        part = jnp.dot(
            active, reduce_ref[:, pl.ds(pl.multiple_of(q_own * 512, 512), 512)], preferred_element_type=F32
        )
        rs_core(s, 1).wait_recv()
        own[s] = part + pcr[s, h]
        rs_core(s, 0).wait_send()
        rs_core(s, 1).wait_send()

    def reduce_wait(s):
        rs_far(s).wait()
        return own[s] + pfr[s].astype(F32)

    for s in range(STREAMS):
        u[s, q_own] = x_ref[rows(s)]
        walk_ref[rows(s)] = x_ref[rows(s)].astype(F32)
    arrived()
    for s in range(STREAMS):
        gather_start(s)

    for s in range(STREAMS):
        noise = bn_ref[rows(s)].astype(F32).reshape(16, 8, 512)
        times = jnp.transpose(jnp.broadcast_to(bt_ref[s : s + 1, :], (128, 128)))
        high = times.astype(BF16).astype(F32)
        low = times - high
        packed = jnp.concatenate([noise[:, :, :256], noise[:, :, 256:]], axis=1)
        clocks = jnp.concatenate([high.reshape(16, 8, 128), low.reshape(16, 8, 128)], axis=1)
        m0[2 * s : 2 * s + 2] = (
            jnp.concatenate([packed, clocks], axis=2).astype(BF16).reshape(2, 2, 4, 16, 384)
        )

    def swap_l():
        return remote(m0.at[:, 1 - l], m1.at[:, l], ms.at[0], mr.at[0], device(z, 1 - l, y, h, c))

    def swap_y(d):
        to = (y + d) % 4
        return remote(m1.at[:, :, to], m2.at[:, :, y], ms.at[d], mr.at[d], device(z, l, to, h, c))

    def swap_z(d):
        to = (z + d) % 4
        return remote(m2.at[to], m3.at[z], ms.at[3 + d], mr.at[3 + d], device(to, l, y, h, c))

    swap_l().start()
    m1[:, l] = m0[:, l]

    loads[0].wait()
    loads[1].wait()
    loads[2].wait()

    def step(k, clock):
        width = steps_ref[k]
        for s in range(STREAMS):
            gather_wait(s)
            normalize(s, bg_ref)
            for n in range(4):
                cols = slice(256 * n, 256 * (n + 1))
                hidden = jnp.dot(nb[...], be[:, cols], preferred_element_type=F32) + clock * bc_ref[:, cols]
                ab[:, cols] = (hidden * jax.nn.sigmoid(hidden)).astype(BF16)
            reduce_start(s, ab[...], br)

        @pl.when(k == 0)
        def _():
            swap_l().wait()
            for d in (1, 2, 3):
                swap_y(d).start()
            m2[:, :, y] = m1[:, :, y]

        @pl.when(k == 1)
        def _():
            for d in (1, 2, 3):
                swap_y(d).wait()
            for d in (1, 2, 3):
                swap_z(d).start()
            m3[z] = m2[z]

        @pl.when(k == 3)
        def _():
            for d in (1, 2, 3):
                swap_z(d).wait()

        spread = jnp.sqrt(jnp.full((1, 512), width, F32)) * NOISE_LEVEL
        for s in range(STREAMS):
            drift = reduce_wait(s)
            state = walk_ref[rows(s)] - width * drift + spread * wn[k, rows(s)].astype(F32)
            walk_ref[rows(s)] = state

            @pl.when(k < 3)
            def _():
                put_own(s, state)

            @pl.when(k == 3)
            def _():
                message = m3[2 * s : 2 * s + 2].reshape(16, 16, 384).astype(F32)
                noise = jnp.concatenate(
                    [message[:, :8, :256].reshape(ROWS, 256), message[:, 8:, :256].reshape(ROWS, 256)], axis=1
                )
                times = (message[:, :8, 256:] + message[:, 8:, 256:]).reshape(ROWS, 128)
                tau[s] = times
                times = jnp.concatenate([times] * 4, axis=1)
                start = state.astype(BF16).astype(F32)
                end = x_ref[rows(s)].astype(F32)
                mixed = (1.0 - times) * start + times * end + jnp.sqrt(times * (1.0 - times)) * NOISE_LEVEL * noise
                flow[s] = (end - mixed) / (1.0 - times)
                put_own(s, mixed)

            gather_start(s)
        return clock - width

    lax.fori_loop(0, 4, step, jnp.float32(1.0))

    loads[3].wait()
    loads[4].wait()
    for s in range(STREAMS):
        gather_wait(s)
        normalize(s, fg_ref)
        normed_ref[rows(s)] = nb[...]
        times = jnp.concatenate([tau[s]] * 2, axis=1)
        for n in range(4):
            cols = slice(256 * n, 256 * (n + 1))
            hidden = jnp.dot(nb[...], fe[:, cols], preferred_element_type=F32) + times * fc_ref[:, cols]
            hid[s, :, cols] = hidden
            act_ref[rows(s), cols] = (hidden * jax.nn.sigmoid(hidden)).astype(BF16)
        reduce_start(s, act_ref[rows(s)], fr)
    scale = 1.0 / (8192.0**0.5)
    for s in range(STREAMS):
        put_own(s, (reduce_wait(s) - flow[s]) * scale)
        gather_start(s)
    for s in range(STREAMS):
        gather_wait(s)
        for q in range(4):
            err_ref[rows(s), 512 * q : 512 * (q + 1)] = u[s, q]
        for n in range(4):
            cols = slice(256 * n, 256 * (n + 1))
            back = lax.dot_general(
                err_ref[rows(s)], fr[cols, :], (((1,), (1,)), ((), ())), preferred_element_type=F32
            )
            hidden = hid[s, :, cols]
            sig = jax.nn.sigmoid(hidden)
            hg_ref[rows(s), cols] = (back * (sig * (1.0 + hidden * (1.0 - sig)))).astype(BF16)
    for s in range(STREAMS):
        ag_core(s).wait_send()
        ag_far(s).wait_send()
        ag_fwd(s).wait_send()


def grad_kernel(
    normed_ref, err_ref, hg_ref, act_ref, ge_ref, gr_ref, g0, g1, r1, a0, a1, r2, b, r3, ss, rs
):
    z, l, y, h, c = place()
    arrived = greet(batch_peers(z, l, y, h, c))

    def ydev(d):
        return device(z, l, (y + d) % 4, h, c)

    def zdev(d):
        return device((z + d) % 4, l, y, h, c)

    def first(p, d, chunk):
        if p == 0:
            to = (y + d) % 4
            return remote(g0.at[chunk, to], r1.at[0, d - 1, chunk], ss.at[0, d - 1], rs.at[0, d - 1], ydev(d))
        to = (z + d) % 4
        return remote(
            g1.at[to, chunk], r1.at[1, d - 1, chunk], ss.at[1, d - 1], rs.at[1, d - 1], zdev(d)
        )

    def first_all(p, d):
        if p == 0:
            return remote(g0.at[:, (y + d) % 4], r1.at[0, d - 1], ss.at[0, d - 1], rs.at[0, d - 1], ydev(d))
        return remote(g1.at[(z + d) % 4], r1.at[1, d - 1], ss.at[1, d - 1], rs.at[1, d - 1], zdev(d))

    def second(p, d):
        if p == 0:
            return remote(a0.at[(z + d) % 4], r2.at[0, d - 1], ss.at[2, d - 1], rs.at[2, d - 1], zdev(d))
        return remote(a1.at[:, (y + d) % 4], r2.at[1, d - 1], ss.at[3, d - 1], rs.at[3, d - 1], ydev(d))

    def third(p):
        return remote(b.at[p, 1 - l], r3.at[p], ss.at[4, p], rs.at[4, p], device(z, 1 - l, y, h, c))

    arrived()

    def make0(i, _):
        left = err_ref[:, pl.ds(pl.multiple_of(i * 256, 256), 256)]
        part = lax.dot_general(left, act_ref[...], (((0,), (0,)), ((), ())), preferred_element_type=F32)
        g0[i] = part.astype(BF16).reshape(4, 64, 1024)
        for d in (1, 2, 3):
            first(0, d, i).start()
        return 0

    lax.fori_loop(0, 8, make0, 0)

    def make1(j, _):
        to = (z + 1 + j // 2) % 4
        half = j % 2
        left = normed_ref[:, pl.ds(pl.multiple_of((to * 2 + half) * 256, 256), 256)]
        part = lax.dot_general(left, hg_ref[...], (((0,), (0,)), ((), ())), preferred_element_type=F32)
        g1[to, pl.ds(half * 4, 4)] = part.astype(BF16).reshape(4, 64, 1024)
        return 0

    for d in (1, 2, 3):
        lax.fori_loop(2 * d - 2, 2 * d, make1, 0)
        first_all(1, d).start()
    lax.fori_loop(6, 8, make1, 0)

    for p in (0, 1):
        for d in (1, 2, 3):
            first_all(p, d).wait()

        def add1(i, _):
            mine = g0[i, y] if p == 0 else g1[z, i]
            total = mine.astype(F32) + sum(r1[p, d, i].astype(F32) for d in range(3))
            if p == 0:
                a0[i // 2, i % 2] = total.astype(BF16)
            else:
                a1[i // 4, i % 4] = total.astype(BF16)
            return 0

        lax.fori_loop(0, 8, add1, 0)
        for d in (1, 2, 3):
            second(p, d).start()
    for p in (0, 1):
        for d in (1, 2, 3):
            second(p, d).wait()
        for i in range(2):
            mine = a0[z, i] if p == 0 else a1[i, y]
            b[p, i] = mine.astype(F32) + sum(r2[p, d, i].astype(F32) for d in range(3))
        third(p).start()
    for p, out in ((0, gr_ref), (1, ge_ref)):
        third(p).wait()
        out[...] = b[p, l] + r3[p]


def body(
    target_latents, walk_noise, step_sizes, back_gain, back_expand, back_clock, back_reduce,
    bridge_times, bridge_noise, fore_gain, fore_expand, fore_clock, fore_reduce,
):
    vmem = pl.BlockSpec(memory_space=pltpu.VMEM)
    smem = pl.BlockSpec(memory_space=pltpu.SMEM)
    hbm = pl.BlockSpec(memory_space=pl.ANY)
    dma = pltpu.SemaphoreType.DMA
    sds = jax.ShapeDtypeStruct
    S, R = STREAMS, ROWS
    walk_end, normed, err, hg, act = pl.pallas_call(
        net_kernel,
        out_shape=(
            sds((256, 512), F32), sds((256, 2048), BF16), sds((256, 2048), BF16),
            sds((256, 1024), BF16), sds((256, 1024), BF16),
        ),
        in_specs=[vmem, hbm, smem, vmem, hbm, vmem, hbm, vmem, vmem, vmem, hbm, vmem, hbm],
        out_specs=(vmem,) * 5,
        scratch_shapes=[
            pltpu.VMEM((2048, 1024), BF16), pltpu.VMEM((1024, 2048), BF16),
            pltpu.VMEM((2048, 1024), BF16), pltpu.VMEM((1024, 2048), BF16),
            pltpu.VMEM((4, 256, 512), BF16),
            pltpu.VMEM((S, 4, R, 512), BF16),
            pltpu.VMEM((R, 2048), BF16), pltpu.VMEM((R, 1024), BF16),
            pltpu.VMEM((S, 2, R, 512), F32), pltpu.VMEM((S, 2, R, 512), F32),
            pltpu.VMEM((S, R, 512), BF16), pltpu.VMEM((S, R, 512), BF16),
            pltpu.VMEM((S, R, 512), F32), pltpu.VMEM((S, R, 512), F32),
            pltpu.VMEM((S, R, 1024), F32), pltpu.VMEM((S, R, 128), F32),
        ]
        + [pltpu.VMEM((4, 2, 4, 16, 384), BF16)] * 4
        + [dma((5,)), dma((6, S)), dma((6, S)), dma((7,)), dma((7,))],
        compiler_params=pltpu.CompilerParams(
            collective_id=0, has_side_effects=True, vmem_limit_bytes=56 * 2**20
        ),
        name="net",
    )(
        target_latents, walk_noise, step_sizes, back_gain.reshape(1, 2048), back_expand,
        back_clock.reshape(1, 1024), back_reduce, bridge_times.reshape(2, 128), bridge_noise,
        fore_gain.reshape(1, 2048), fore_expand, fore_clock.reshape(1, 1024), fore_reduce,
    )
    grad_expand, grad_reduce_t = pl.pallas_call(
        grad_kernel,
        out_shape=(sds((64, 1024), F32), sds((64, 1024), F32)),
        in_specs=[vmem] * 4,
        out_specs=(vmem, vmem),
        scratch_shapes=[
            pltpu.VMEM((8, 4, 64, 1024), BF16), pltpu.VMEM((4, 8, 64, 1024), BF16),
            pltpu.VMEM((2, 3, 8, 64, 1024), BF16),
            pltpu.VMEM((4, 2, 64, 1024), BF16), pltpu.VMEM((2, 4, 64, 1024), BF16),
            pltpu.VMEM((2, 3, 2, 64, 1024), BF16),
            pltpu.VMEM((2, 2, 64, 1024), F32), pltpu.VMEM((2, 64, 1024), F32),
            dma((5, 3)), dma((5, 3)),
        ],
        compiler_params=pltpu.CompilerParams(
            collective_id=1, has_side_effects=True, vmem_limit_bytes=56 * 2**20
        ),
        name="grad",
    )(normed, err, hg, act)
    return walk_end, grad_expand, grad_reduce_t


def solution(mesh):
    placed = (
        P("batch", "tensor"), P(None, "batch", "tensor"), P(), P(), P(None, "tensor"), P("tensor"),
        P("tensor", None), P("batch"), P("batch", "tensor"), P(), P(None, "tensor"), P("tensor"),
        P("tensor", None),
    )
    return jax.shard_map(
        body, mesh=mesh, in_specs=placed,
        out_specs=(P("batch", "tensor"), P("batch", "tensor"), P("batch", "tensor")), check_vma=False,
    )
```

time: 647 us -> 190 us (0.29)
  waiting for transfers between devices: 513 us -> 0 us
  Pallas kernels: 0 us -> 184 us
  matrix products: 47 us -> 0 us
  other arithmetic: 28.8 us -> 0 us
  between operations: 19.2 us -> 0.65 us
  local copies, waits for them, and re-layouts: 22.2 us -> 5.21 us
  starting transfers between devices: 15.4 us -> 0 us
    unnamed x13 -> x0, waiting for transfers between devices: 204 us -> none
    pallas_call x0 -> x2, Pallas kernels: none -> 184 us  [the longest x1 102 us: body(): pl.pallas_call(net_kernel, out_shape=(sds((256, 512), F32), sds((256, 204...]
    reduce_scatter x5 -> x0, waiting for transfers between devices: 179 us -> none  [the longest x4 141 us: body(): lax.psum_scatter(partial_drift, 'tensor', scatter_dimension=1, tiled=True)]
    all_gather x6 -> x0, waiting for transfers between devices: 121 us -> none  [the longest x4 83.9 us: body(): lax.all_gather(walk_state.astype(jnp.bfloat16), 'tensor', axis=1, tiled=T...]
    dot_general x8 -> x0, matrix products: 47 us -> none  [the longest x4 30.5 us: body(): jnp.dot(active, back_reduce, preferred_element_type=jnp.float32)]
    all_to_all x2 -> x0, starting transfers between devices: 14.7 us -> none  [the longest x1 7.42 us: body(): lax.all_to_all(target_latents, 'batch', split_axis=0, concat_axis=0, tile...]
    unnamed x29 -> x3, local copies, waits for them, and re-layouts: 19.7 us -> 5.21 us
    convert_element_type x5 -> x0, other arithmetic: 11.5 us -> none  [the longest x3 8.46 us: body(): walk_state.astype(jnp.bfloat16)]
  transfers between devices with their start and end apart: 14 -> 0, of which waited for: 13 -> 0; matrix products, arithmetic and copies ran while one was open for 1% -> 0% of each run, Pallas kernels for 0% -> 0%
where the time goes in v1:
time: 190 us
  Pallas kernels  184 us (97%)
  local copies, waits for them, and re-layouts  5.21 us (3%)
    pallas_call x1, Pallas kernels, body(): pl.pallas_call(net_kernel, out_shape=(sds((256, 512), F32), sds((256, 204...  102 us
    pallas_call x1, Pallas kernels, body(): pl.pallas_call(grad_kernel, out_shape=(sds((64, 1024), F32), sds((64, 102...  81.5 us
    unnamed x3, local copies, waits for them, and re-layouts  5.21 us

profile of v1, /device:TPU:0, one launch (start us, length us, event | category | flops | bytes accessed | tf_op | source)
XLA Modules:
  0.0 189.7 jit_solution(7243302780130991160)
XLA Ops:
  0.6 102.3 %net.1 = (f32[256,512]{1,0:T(8,128)}, bf16[256,2048]{1,0:T(8,128)(2,1)}, bf16[256,2048]{1,0:T(8,128)(2,1)}, bf16[256,1024]{1,0:T(8,128)(2,1)}, bf16[256,1024]{1,0:T(8,128)(2,1)}) custom-call(bf16[256,512]{1,0:T(8,128)(2,1)} %x_ref.1, bf16[4,256,512]{2,1,0:T(8,128)(2,1)} %wn_hbm.1, f32[4]{0:T(128)} %steps_ref.1, f32[1,2048]{1,0:T(1,128)} %bitcast.5, ...), custom_call_target="tpu_custom_call" | custom-call | tf_op jit(solution)/shard_map/net/pallas_call | solution.py:361
  103.0 81.5 %grad.1 = (f32[64,1024]{1,0:T(8,128)}, f32[64,1024]{1,0:T(8,128)}) custom-call(bf16[256,2048]{1,0:T(8,128)(2,1)} %get-tuple-element.11.normed_ref, bf16[256,2048]{1,0:T(8,128)(2,1)} %get-tuple-element.12.err_ref, bf16[256,1024]{1,0:T(8,128)(2,1)} %get-tuple-element.13.hg_ref, bf16[256,1024]{1,0:T(8,128)(2,1)} %get-tuple-element.14.act_ref), custom_call_target="tpu_custom_call" | custom-call | tf_op jit(solution)/shard_map/grad/pallas_call | solution.py:391
  184.5 1.9 copy.19
  186.4 1.7 copy.20
  188.0 1.7 copy.21

commit v2 on v1

--- a/solution.py
+++ b/solution.py
@@ -46,9 +46,12 @@
 
 def net_kernel(
     x_ref, wn_hbm, steps_ref, bg_ref, be_hbm, bc_ref, br_hbm, bt_ref, bn_ref, fg_ref, fe_hbm, fc_ref, fr_hbm,
-    walk_ref, normed_ref, err_ref, hg_ref, act_ref,
+    walk_ref, ge_ref, gr_ref,
     be, br, fe, fr, wn, u, nb, ab, pcs, pcr, pfs, pfr, own, flow, hid, tau, m0, m1, m2, m3,
-    load_sem, ss, rs, ms, mr,
+    err_ref, normh, act_ref, hg_ref, pn, ph,
+    gy_r, gz_r, r1y_r, r1z_r, ay_r, az_r, r2_r, b_r, s_r, r3_r,
+    gy_e, gz_e, r1y_e, r1z_e, ay_e, az_e, r2_e,
+    load_sem, ss, rs, ms, mr, gs, gr,
 ):
     z, l, y, h, c = place()
     core_dev = device(z, l, y, h, 1 - c)
@@ -231,7 +234,9 @@
     for s in range(STREAMS):
         gather_wait(s)
         normalize(s, fg_ref)
-        normed_ref[rows(s)] = nb[...]
+        for q in range(4):
+            for i in range(2):
+                normh[i, rows(s), 256 * q : 256 * (q + 1)] = nb[:, 512 * q + 256 * i : 512 * q + 256 * (i + 1)]
         times = jnp.concatenate([tau[s]] * 2, axis=1)
         for n in range(4):
             cols = slice(256 * n, 256 * (n + 1))
@@ -247,6 +252,77 @@
         gather_wait(s)
         for q in range(4):
             err_ref[rows(s), 512 * q : 512 * (q + 1)] = u[s, q]
+
+    pair_dev = device(z, 1 - l, y, h, c)
+    share = pl.ds(pl.multiple_of(c * 128, 128), 128)
+
+    def ydev(d):
+        return device(z, l, (y + d) % 4, h, c)
+
+    def zdev(d):
+        return device((z + d) % 4, l, y, h, c)
+
+    def pair_normed():
+        return remote(normh.at[1 - l, share], pn.at[share], gs.at[26], gr.at[26], pair_dev)
+
+    def pair_forward():
+        return remote(pn.at[share], pn.at[share], gs.at[27], gr.at[27], core_dev)
+
+    def pair_grad(s):
+        return remote(hg_ref.at[rows(s)], ph.at[rows(s)], gs.at[28 + s], gr.at[28 + s], pair_dev)
+
+    def r_first_y(d):
+        return remote(gy_r.at[:, :, (y + d) % 4], r1y_r.at[d - 1], gs.at[d - 1], gr.at[d - 1], ydev(d))
+
+    def r_first_z(d):
+        return remote(gz_r.at[(z + d) % 4], r1z_r.at[d - 1], gs.at[2 + d], gr.at[2 + d], zdev(d))
+
+    def r_second_y(d):
+        return remote(ay_r.at[(z + d) % 4], r2_r.at[0, d - 1], gs.at[5 + d], gr.at[5 + d], zdev(d))
+
+    def r_second_z(d):
+        return remote(az_r.at[:, (y + d) % 4], r2_r.at[1, d - 1], gs.at[8 + d], gr.at[8 + d], ydev(d))
+
+    def r_third(i):
+        return remote(s_r.at[i], r3_r.at[i], gs.at[12 + i], gr.at[12 + i], pair_dev)
+
+    def e_first_y(d):
+        return remote(gy_e.at[:, (y + d) % 4], r1y_e.at[d - 1], gs.at[13 + d], gr.at[13 + d], ydev(d))
+
+    def e_first_z(d):
+        return remote(gz_e.at[(z + d) % 4], r1z_e.at[d - 1], gs.at[16 + d], gr.at[16 + d], zdev(d))
+
+    def e_second_y(d):
+        return remote(ay_e.at[(z + d) % 4], r2_e.at[0, d - 1], gs.at[19 + d], gr.at[19 + d], zdev(d))
+
+    def e_second_z(d):
+        return remote(az_e.at[(y + d) % 4], r2_e.at[1, d - 1], gs.at[22 + d], gr.at[22 + d], ydev(d))
+
+    def outer(left, right):
+        return lax.dot_general(left, right, (((0,), (0,)), ((), ())), preferred_element_type=F32)
+
+    def make_r(to):
+        def one(i, _):
+            column = pl.multiple_of((to * 2 + i) * 256, 256)
+            part = outer(err_ref[:, pl.ds(column, 256)], act_ref[...]).astype(BF16)
+            gy_r[to, i] = part[:, :512].reshape(4, 64, 512)
+            gz_r[to, i] = part[:, 512:].reshape(4, 64, 512)
+            for d in (1, 2, 3):
+                dst = (y + d) % 4
+                remote(
+                    gy_r.at[to, i, dst], r1y_r.at[d - 1, to, i], gs.at[d - 1], gr.at[d - 1], ydev(d)
+                ).start()
+            return 0
+
+        lax.fori_loop(0, 2, one, 0)
+
+    pair_normed().start()
+    for d in (2, 1, 3, 0):
+        make_r((z + d) % 4)
+        if d:
+            r_first_z(d).start()
+
+    for s in range(STREAMS):
         for n in range(4):
             cols = slice(256 * n, 256 * (n + 1))
             back = lax.dot_general(
@@ -255,97 +331,118 @@
             hidden = hid[s, :, cols]
             sig = jax.nn.sigmoid(hidden)
             hg_ref[rows(s), cols] = (back * (sig * (1.0 + hidden * (1.0 - sig)))).astype(BF16)
+        pair_grad(s).start()
     for s in range(STREAMS):
         ag_core(s).wait_send()
         ag_far(s).wait_send()
         ag_fwd(s).wait_send()
 
-
-def grad_kernel(
-    normed_ref, err_ref, hg_ref, act_ref, ge_ref, gr_ref, g0, g1, r1, a0, a1, r2, b, r3, ss, rs
-):
-    z, l, y, h, c = place()
-    arrived = greet(batch_peers(z, l, y, h, c))
-
-    def ydev(d):
-        return device(z, l, (y + d) % 4, h, c)
-
-    def zdev(d):
-        return device((z + d) % 4, l, y, h, c)
-
-    def first(p, d, chunk):
-        if p == 0:
-            to = (y + d) % 4
-            return remote(g0.at[chunk, to], r1.at[0, d - 1, chunk], ss.at[0, d - 1], rs.at[0, d - 1], ydev(d))
-        to = (z + d) % 4
-        return remote(
-            g1.at[to, chunk], r1.at[1, d - 1, chunk], ss.at[1, d - 1], rs.at[1, d - 1], zdev(d)
-        )
-
-    def first_all(p, d):
-        if p == 0:
-            return remote(g0.at[:, (y + d) % 4], r1.at[0, d - 1], ss.at[0, d - 1], rs.at[0, d - 1], ydev(d))
-        return remote(g1.at[(z + d) % 4], r1.at[1, d - 1], ss.at[1, d - 1], rs.at[1, d - 1], zdev(d))
-
-    def second(p, d):
-        if p == 0:
-            return remote(a0.at[(z + d) % 4], r2.at[0, d - 1], ss.at[2, d - 1], rs.at[2, d - 1], zdev(d))
-        return remote(a1.at[:, (y + d) % 4], r2.at[1, d - 1], ss.at[3, d - 1], rs.at[3, d - 1], ydev(d))
-
-    def third(p):
-        return remote(b.at[p, 1 - l], r3.at[p], ss.at[4, p], rs.at[4, p], device(z, 1 - l, y, h, c))
-
-    arrived()
-
-    def make0(i, _):
-        left = err_ref[:, pl.ds(pl.multiple_of(i * 256, 256), 256)]
-        part = lax.dot_general(left, act_ref[...], (((0,), (0,)), ((), ())), preferred_element_type=F32)
-        g0[i] = part.astype(BF16).reshape(4, 64, 1024)
+    pair_normed().wait()
+    pair_forward().start()
+    pair_forward().wait()
+    for s in range(STREAMS):
+        pair_grad(s).wait()
+
+    def make_e(j, _):
+        to = (z + 1 + j) % 4
+        column = pl.ds(pl.multiple_of(to * 256, 256), 256)
+        part = (outer(normh[l, :, column], hg_ref[...]) + outer(pn[:, column], ph[...])).astype(BF16)
+        gy_e[to] = part[:, :512].reshape(4, 64, 512)
+        gz_e[to] = part[:, 512:].reshape(4, 64, 512)
         for d in (1, 2, 3):
-            first(0, d, i).start()
+            dst = (y + d) % 4
+            remote(
+                gy_e.at[to, dst], r1y_e.at[d - 1, to], gs.at[13 + d], gr.at[13 + d], ydev(d)
+            ).start()
         return 0
 
-    lax.fori_loop(0, 8, make0, 0)
-
-    def make1(j, _):
-        to = (z + 1 + j // 2) % 4
-        half = j % 2
-        left = normed_ref[:, pl.ds(pl.multiple_of((to * 2 + half) * 256, 256), 256)]
-        part = lax.dot_general(left, hg_ref[...], (((0,), (0,)), ((), ())), preferred_element_type=F32)
-        g1[to, pl.ds(half * 4, 4)] = part.astype(BF16).reshape(4, 64, 1024)
+    for d in (1, 2, 3):
+        lax.fori_loop(d - 1, d, make_e, 0)
+        e_first_z(d).start()
+    lax.fori_loop(3, 4, make_e, 0)
+
+    for d in (1, 2, 3):
+        r_first_y(d).wait()
+
+    def add_ry(i, _):
+        total = gy_r[i, :, y].astype(F32) + sum(r1y_r[d, i].astype(F32) for d in range(3))
+        ay_r[i] = total.astype(BF16)
         return 0
 
-    for d in (1, 2, 3):
-        lax.fori_loop(2 * d - 2, 2 * d, make1, 0)
-        first_all(1, d).start()
-    lax.fori_loop(6, 8, make1, 0)
-
-    for p in (0, 1):
+    lax.fori_loop(0, 4, add_ry, 0)
+    for d in (1, 2, 3):
+        r_second_y(d).start()
+    for d in (1, 2, 3):
+        r_first_z(d).wait()
+
+    def add_rz(i, _):
+        total = gz_r[z, :, i].astype(F32) + sum(r1z_r[d, :, i].astype(F32) for d in range(3))
+        az_r[:, i] = total.astype(BF16)
+        return 0
+
+    lax.fori_loop(0, 4, add_rz, 0)
+    for d in (1, 2, 3):
+        r_second_z(d).start()
+
+    def finish_r(i):
         for d in (1, 2, 3):
-            first_all(p, d).wait()
-
-        def add1(i, _):
-            mine = g0[i, y] if p == 0 else g1[z, i]
-            total = mine.astype(F32) + sum(r1[p, d, i].astype(F32) for d in range(3))
-            if p == 0:
-                a0[i // 2, i % 2] = total.astype(BF16)
-            else:
-                a1[i // 4, i % 4] = total.astype(BF16)
-            return 0
-
-        lax.fori_loop(0, 8, add1, 0)
+            (r_second_y(d) if i == 0 else r_second_z(d)).wait()
+
+        def own(side):
+            return ay_r[z, side] if i == 0 else az_r[side, y]
+
+        s_r[i] = (
+            own(1 - l).astype(F32) + sum(r2_r[i, d, 1 - l].astype(F32) for d in range(3))
+        ).astype(BF16)
+        r_third(i).start()
+        b_r[i] = own(l).astype(F32) + sum(r2_r[i, d, l].astype(F32) for d in range(3))
+
+    finish_r(0)
+    finish_r(1)
+
+    for d in (1, 2, 3):
+        e_first_y(d).wait()
+
+    def add_ey(i, _):
+        total = gy_e[i, y].astype(F32) + sum(r1y_e[d, i].astype(F32) for d in range(3))
+        ay_e[i] = total.astype(BF16)
+        return 0
+
+    lax.fori_loop(0, 4, add_ey, 0)
+    for d in (1, 2, 3):
+        e_second_y(d).start()
+    for d in (1, 2, 3):
+        e_first_z(d).wait()
+
+    def add_ez(i, _):
+        total = gz_e[z, i].astype(F32) + sum(r1z_e[d, i].astype(F32) for d in range(3))
+        az_e[i] = total.astype(BF16)
+        return 0
+
+    lax.fori_loop(0, 4, add_ez, 0)
+    for d in (1, 2, 3):
+        e_second_z(d).start()
+    for i in range(2):
+        r_third(i).wait()
+        gr_ref[:, 512 * i : 512 * (i + 1)] = b_r[i] + r3_r[i].astype(F32)
+    for i in range(2):
         for d in (1, 2, 3):
-            second(p, d).start()
-    for p in (0, 1):
-        for d in (1, 2, 3):
-            second(p, d).wait()
-        for i in range(2):
-            mine = a0[z, i] if p == 0 else a1[i, y]
-            b[p, i] = mine.astype(F32) + sum(r2[p, d, i].astype(F32) for d in range(3))
-        third(p).start()
-    for p, out in ((0, gr_ref), (1, ge_ref)):
-        third(p).wait()
-        out[...] = b[p, l] + r3[p]
+            (e_second_y(d) if i == 0 else e_second_z(d)).wait()
+        mine = ay_e[z] if i == 0 else az_e[y]
+        ge_ref[:, 512 * i : 512 * (i + 1)] = mine.astype(F32) + sum(r2_e[i, d].astype(F32) for d in range(3))
+
+
+def copy_kernel(a_in, b_in, c_in, a_out, b_out, c_out, a_mid, b_mid, c_mid, sems):
+    trios = ((a_in, a_mid, a_out), (b_in, b_mid, b_out), (c_in, c_mid, c_out))
+    into = [pltpu.make_async_copy(src, mid, sems.at[0, i]) for i, (src, mid, dst) in enumerate(trios)]
+    out = [pltpu.make_async_copy(mid, dst, sems.at[1, i]) for i, (src, mid, dst) in enumerate(trios)]
+    for copy in into:
+        copy.start()
+    for first, second in zip(into, out):
+        first.wait()
+        second.start()
+    for copy in out:
+        copy.wait()
 
 
 def body(
@@ -358,14 +455,11 @@
     dma = pltpu.SemaphoreType.DMA
     sds = jax.ShapeDtypeStruct
     S, R = STREAMS, ROWS
-    walk_end, normed, err, hg, act = pl.pallas_call(
+    outs = pl.pallas_call(
         net_kernel,
-        out_shape=(
-            sds((256, 512), F32), sds((256, 2048), BF16), sds((256, 2048), BF16),
-            sds((256, 1024), BF16), sds((256, 1024), BF16),
-        ),
+        out_shape=(sds((256, 512), F32), sds((64, 1024), F32), sds((64, 1024), F32)),
         in_specs=[vmem, hbm, smem, vmem, hbm, vmem, hbm, vmem, vmem, vmem, hbm, vmem, hbm],
-        out_specs=(vmem,) * 5,
+        out_specs=(vmem,) * 3,
         scratch_shapes=[
             pltpu.VMEM((2048, 1024), BF16), pltpu.VMEM((1024, 2048), BF16),
             pltpu.VMEM((2048, 1024), BF16), pltpu.VMEM((1024, 2048), BF16),
@@ -378,9 +472,23 @@
             pltpu.VMEM((S, R, 1024), F32), pltpu.VMEM((S, R, 128), F32),
         ]
         + [pltpu.VMEM((4, 2, 4, 16, 384), BF16)] * 4
-        + [dma((5,)), dma((6, S)), dma((6, S)), dma((7,)), dma((7,))],
+        + [
+            pltpu.VMEM((256, 2048), BF16), pltpu.VMEM((2, 256, 1024), BF16),
+            pltpu.VMEM((256, 1024), BF16), pltpu.VMEM((256, 1024), BF16),
+            pltpu.VMEM((256, 1024), BF16), pltpu.VMEM((256, 1024), BF16),
+            pltpu.VMEM((4, 2, 4, 64, 512), BF16), pltpu.VMEM((4, 2, 4, 64, 512), BF16),
+            pltpu.VMEM((3, 4, 2, 64, 512), BF16), pltpu.VMEM((3, 2, 4, 64, 512), BF16),
+            pltpu.VMEM((4, 2, 64, 512), BF16), pltpu.VMEM((2, 4, 64, 512), BF16),
+            pltpu.VMEM((2, 3, 2, 64, 512), BF16),
+            pltpu.VMEM((2, 64, 512), F32), pltpu.VMEM((2, 64, 512), BF16), pltpu.VMEM((2, 64, 512), BF16),
+            pltpu.VMEM((4, 4, 64, 512), BF16), pltpu.VMEM((4, 4, 64, 512), BF16),
+            pltpu.VMEM((3, 4, 64, 512), BF16), pltpu.VMEM((3, 4, 64, 512), BF16),
+            pltpu.VMEM((4, 64, 512), BF16), pltpu.VMEM((4, 64, 512), BF16),
+            pltpu.VMEM((2, 3, 64, 512), BF16),
+        ]
+        + [dma((5,)), dma((6, S)), dma((6, S)), dma((7,)), dma((7,)), dma((30,)), dma((30,))],
         compiler_params=pltpu.CompilerParams(
-            collective_id=0, has_side_effects=True, vmem_limit_bytes=56 * 2**20
+            collective_id=0, has_side_effects=True, vmem_limit_bytes=58 * 2**20
         ),
         name="net",
     )(
@@ -388,25 +496,14 @@
         back_clock.reshape(1, 1024), back_reduce, bridge_times.reshape(2, 128), bridge_noise,
         fore_gain.reshape(1, 2048), fore_expand, fore_clock.reshape(1, 1024), fore_reduce,
     )
-    grad_expand, grad_reduce_t = pl.pallas_call(
-        grad_kernel,
-        out_shape=(sds((64, 1024), F32), sds((64, 1024), F32)),
-        in_specs=[vmem] * 4,
-        out_specs=(vmem, vmem),
-        scratch_shapes=[
-            pltpu.VMEM((8, 4, 64, 1024), BF16), pltpu.VMEM((4, 8, 64, 1024), BF16),
-            pltpu.VMEM((2, 3, 8, 64, 1024), BF16),
-            pltpu.VMEM((4, 2, 64, 1024), BF16), pltpu.VMEM((2, 4, 64, 1024), BF16),
-            pltpu.VMEM((2, 3, 2, 64, 1024), BF16),
-            pltpu.VMEM((2, 2, 64, 1024), F32), pltpu.VMEM((2, 64, 1024), F32),
-            dma((5, 3)), dma((5, 3)),
-        ],
-        compiler_params=pltpu.CompilerParams(
-            collective_id=1, has_side_effects=True, vmem_limit_bytes=56 * 2**20
-        ),
-        name="grad",
-    )(normed, err, hg, act)
-    return walk_end, grad_expand, grad_reduce_t
+    return pl.pallas_call(
+        copy_kernel,
+        out_shape=tuple(sds(o.shape, o.dtype) for o in outs),
+        in_specs=[hbm] * 3,
+        out_specs=(hbm,) * 3,
+        scratch_shapes=[pltpu.VMEM(o.shape, o.dtype) for o in outs] + [dma((2, 3))],
+        name="place_outputs",
+    )(*outs)
 
 
 def solution(mesh):

time: 190 us -> 154 us (0.81)
  Pallas kernels: 184 us -> 153 us
  local copies, waits for them, and re-layouts: 5.21 us -> 0 us
    pallas_call x2, Pallas kernels: 184 us -> 153 us  [the longest x1 151 us: body(): pl.pallas_call(net_kernel, out_shape=(sds((256, 512), F32), sds((64, 1024...]
    unnamed x3 -> x0, local copies, waits for them, and re-layouts: 5.21 us -> none
where the time goes in v2:
time: 154 us
  Pallas kernels  153 us (99%)
    pallas_call x1, Pallas kernels, body(): pl.pallas_call(net_kernel, out_shape=(sds((256, 512), F32), sds((64, 1024...  151 us

profile of v2, /device:TPU:0, one launch (start us, length us, event | category | flops | bytes accessed | tf_op | source)
XLA Modules:
  0.0 153.8 jit_solution(14039575588133016253)
XLA Ops:
  0.6 151.1 %net.1 = (f32[256,512]{1,0:T(8,128)}, f32[64,1024]{1,0:T(8,128)}, f32[64,1024]{1,0:T(8,128)}) custom-call(bf16[256,512]{1,0:T(8,128)(2,1)} %x_ref.1, bf16[4,256,512]{2,1,0:T(8,128)(2,1)} %wn_hbm.1, f32[4]{0:T(128)} %steps_ref.1, f32[1,2048]{1,0:T(1,128)} %bitcast.5, bf16[2048,1024]{1,0:T(8,128)(2,1)} %be_hbm.1, f32[1,1024]{1,0:T(1,128)} %bitcast.7, ...), custom_call_target="tpu_custom_call" | custom-call | tf_op jit(solution)/shard_map/net/pallas_call | solution.py:458
  151.8 2.1 %place_outputs.1 = (f32[256,512]{1,0:T(8,128)}, f32[64,1024]{1,0:T(8,128)}, f32[64,1024]{1,0:T(8,128)}) custom-call(f32[256,512]{1,0:T(8,128)} %get-tuple-element.6.a_in, f32[64,1024]{1,0:T(8,128)} %get-tuple-element.7.b_in, f32[64,1024]{1,0:T(8,128)} %get-tuple-element.8.c_in), custom_call_target="tpu_custom_call" | custom-call | tf_op jit(solution)/shard_map/place_outputs/pallas_call | solution.py:499

commit v3 on v2

v3 whole, which is shorter than its diff:
```python
import jax
import jax.numpy as jnp
from jax import lax
from jax.experimental import pallas as pl
from jax.experimental.pallas import tpu as pltpu
from jax.sharding import PartitionSpec as P

NOISE_LEVEL = 0.5
EPSILON = 1e-06
MESH = pl.DeviceIdType.MESH
F32 = jnp.float32
BF16 = jnp.bfloat16
ROWS = 128


def place():
    b = lax.axis_index("batch")
    t = lax.axis_index("tensor")
    return b // 8, (b // 4) % 2, b % 4, t // 2, t % 2


def device(z, l, y, h, c):
    return (z * 8 + l * 4 + y, h * 2 + c)


def remote(src, dst, send_sem, recv_sem, dev):
    return pltpu.make_async_remote_copy(
        src_ref=src, dst_ref=dst, send_sem=send_sem, recv_sem=recv_sem, device_id=dev, device_id_type=MESH
    )


def greet(devices):
    barrier = pltpu.get_barrier_semaphore()
    for dev in devices:
        pl.semaphore_signal(barrier, inc=1, device_id=dev, device_id_type=MESH)
    return lambda: pl.semaphore_wait(barrier, len(devices))


def batch_peers(z, l, y, h, c):
    peers = [device(z, 1 - l, y, h, c)]
    peers += [device(z, l, (y + d) % 4, h, c) for d in (1, 2, 3)]
    peers += [device((z + d) % 4, l, y, h, c) for d in (1, 2, 3)]
    return peers


def net_kernel(
    x_ref, wn_hbm, steps_ref, bg_ref, be_hbm, bc_ref, br_hbm, bt_ref, bn_ref, fg_ref, fe_hbm, fc_ref, fr_hbm,
    walk_ref, ge_ref, gr_ref,
    be, br, fe, fr, bca, fca, wn, xt, u, st, acc, ab, own, pfs, pfr, flow, m0, m1, m2, m3, mf, wx,
    err, normh, act_ref, hg_ref, hs, pn, ph,
    gy_r, gz_r, r1y_r, r1z_r, ay_r, az_r, r2_r, b_r, s_r, r3_r,
    gy_e, gz_e, r1y_e, r1z_e, ay_e, az_e, r2_e,
    load_sem, cs, cr, fs, fr_sem, ms, mr, gs, gr,
):
    z, l, y, h, c = place()
    core_dev = device(z, l, y, h, 1 - c)
    far_dev = device(z, l, y, 1 - h, c)
    pair_dev = device(z, 1 - l, y, h, c)
    share = pl.ds(pl.multiple_of(c * 128, 128), 128)
    other = pl.ds(pl.multiple_of((1 - c) * 128, 128), 128)

    def load(i):
        src, dst = (
            (be_hbm, be.at[c]), (br_hbm, br.at[c]), (fe_hbm, fe.at[c]), (fr_hbm, fr.at[c]),
            (wn_hbm.at[:, share], wn.at[c]),
        )[i]
        return pltpu.make_async_copy(src, dst, load_sem.at[i])

    def cross(i):
        src, dst = (
            (be_hbm, be.at[c]), (br_hbm, br.at[c]), (fe_hbm, fe.at[c]), (fr_hbm, fr.at[c]),
            (wn_hbm.at[:, other], wn.at[c]),
            (x_ref.at[other], xt.at[c]),
            (bca.at[c], bca.at[c]), (fca.at[c], fca.at[c]),
            (m3.at[pl.ds(2 * (1 - c), 2)], mf.at[c]),
            (st.at[pl.ds(2 * (1 - c), 2)], wx),
            (ab.at[1 - c], act_ref.at[share]),
            (normh.at[:, share], normh.at[:, share]),
            (hs, hg_ref.at[share]),
        )[i]
        return remote(src, dst, cs.at[i], cr.at[i], core_dev)

    def cross_err(j, i):
        return remote(err.at[j, share], err.at[j, share], cs.at[13 + i], cr.at[13 + i], core_dev)

    def gather(i):
        return remote(u.at[4 * h + i], u.at[4 * h + i], fs.at[i], fr_sem.at[i], far_dev)

    def reduce(i):
        return remote(pfs.at[i], pfr.at[i], fs.at[4 + i], fr_sem.at[4 + i], far_dev)

    def gather_err(i):
        j = 4 * h + i
        return remote(err.at[j, share], err.at[j, share], fs.at[8 + i], fr_sem.at[8 + i], far_dev)

    for i in (0, 1, 4):
        load(i).start()
    arrived = greet([core_dev, far_dev] + batch_peers(z, l, y, h, c))
    bca[c] = bc_ref[...]
    fca[c] = fc_ref[...]
    for i in range(2):
        u[4 * h + 2 * c + i] = x_ref[share, 256 * i : 256 * (i + 1)]
    xt[c] = x_ref[share]
    arrived()
    cross(5).start()
    for i in range(2):
        gather(2 * c + i).start()
    cross(6).start()
    cross(0).start()
    cross(7).start()
    cross(5).wait()
    for i in range(2):
        u[4 * h + 2 * (1 - c) + i] = xt[1 - c, :, 256 * i : 256 * (i + 1)]
        gather(2 * (1 - c) + i).start()
    cross(1).start()
    cross(4).start()
    for i in range(4):
        st[i] = u[4 * h + i].astype(F32)

    for s in range(2):
        noise = bn_ref[128 * s : 128 * (s + 1)].astype(F32).reshape(16, 8, 512)
        times = jnp.transpose(jnp.broadcast_to(bt_ref[s : s + 1, :], (128, 128)))
        high = times.astype(BF16).astype(F32)
        low = times - high
        packed = jnp.concatenate([noise[:, :, :256], noise[:, :, 256:]], axis=1)
        clocks = jnp.concatenate([high.reshape(16, 8, 128), low.reshape(16, 8, 128)], axis=1)
        m0[2 * s : 2 * s + 2] = (
            jnp.concatenate([packed, clocks], axis=2).astype(BF16).reshape(2, 2, 4, 16, 384)
        )

    def swap_l():
        return remote(m0.at[:, 1 - l], m1.at[:, l], ms.at[0], mr.at[0], pair_dev)

    def swap_y(d):
        to = (y + d) % 4
        return remote(m1.at[:, :, to], m2.at[:, :, y], ms.at[d], mr.at[d], device(z, l, to, h, c))

    def swap_z(d):
        to = (z + d) % 4
        return remote(m2.at[to], m3.at[z], ms.at[3 + d], mr.at[3 + d], device(to, l, y, h, c))

    swap_l().start()
    m1[:, l] = m0[:, l]

    def scaled(j, gain_ref):
        rows = u[j].astype(F32)
        return jnp.sum(rows * rows, axis=1, keepdims=True), (rows * gain_ref[j]).astype(BF16)

    def expand(gain_ref, weights, finish):
        squares = jnp.zeros((ROWS, 1), F32)
        near = []
        for i in range(4):
            square, part = scaled(4 * h + i, gain_ref)
            squares += square
            near.append(part)
        near = jnp.concatenate(near, axis=1)
        near_rows = pl.ds(pl.multiple_of(h * 1024, 1024), 1024)
        for q in range(2):
            for n in range(4):
                cols = slice(256 * n, 256 * (n + 1))
                acc[q, :, cols] = jnp.dot(near, weights[q, near_rows, cols], preferred_element_type=F32)
        for i in range(4):
            gather(i).wait_recv()
            j = 4 * (1 - h) + i
            square, part = scaled(j, gain_ref)
            squares += square
            far_rows = pl.ds(pl.multiple_of(j * 256, 256), 256)
            if i == 3:
                factor = lax.rsqrt(squares * (1.0 / 2048.0) + EPSILON)
            for q in range(2):
                for n in range(4):
                    cols = slice(256 * n, 256 * (n + 1))
                    total = acc[q, :, cols] + jnp.dot(part, weights[q, far_rows, cols], preferred_element_type=F32)
                    if i < 3:
                        acc[q, :, cols] = total
                    else:
                        finish(q, cols, total * factor)
        return factor

    def contract(weights, j):
        cols = pl.ds(pl.multiple_of(j * 256, 256), 256)
        return jnp.dot(ab[0], weights[0, :, cols], preferred_element_type=F32) + jnp.dot(
            ab[1], weights[1, :, cols], preferred_element_type=F32
        )

    def reduce_start(weights):
        for i in range(4):
            pfs[i] = contract(weights, 4 * (1 - h) + i).astype(BF16)
            reduce(i).start()
        for i in range(4):
            own[i] = contract(weights, 4 * h + i)

    def reduce_wait(i):
        reduce(i).wait()
        return own[i] + pfr[i].astype(F32)

    for i in (0, 1, 4):
        load(i).wait()
    cross(0).wait()
    cross(6).wait()
    cross(7).wait()

    def step(k, clock):
        width = steps_ref[k]

        def finish(q, cols, product):
            hidden = product + clock * bca[q, :, cols]
            ab[q, :, cols] = (hidden * jax.nn.sigmoid(hidden)).astype(BF16)

        expand(bg_ref, be, finish)

        @pl.when(k == 0)
        def _():
            cross(1).wait()

        reduce_start(br)

        @pl.when(k == 0)
        def _():
            cross(4).wait()
            for i in (2, 3):
                load(i).start()
            cross(2).start()
            swap_l().wait()
            for d in (1, 2, 3):
                swap_y(d).start()
            m2[:, :, y] = m1[:, :, y]

        @pl.when(k == 1)
        def _():
            cross(3).start()
            for d in (1, 2, 3):
                swap_y(d).wait()
            for d in (1, 2, 3):
                swap_z(d).start()
            m3[z] = m2[z]

        @pl.when(k == 2)
        def _():
            for d in (1, 2, 3):
                swap_z(d).wait()
            cross(8).start()
            mf[c] = m3[pl.ds(2 * c, 2)]

        @pl.when(k == 3)
        def _():
            cross(8).wait()

        spread = jnp.sqrt(jnp.full((1, 256), width, F32)) * NOISE_LEVEL
        for i in range(4):
            q, cols = i // 2, slice(256 * (i % 2), 256 * (i % 2) + 256)
            state = st[i] - width * reduce_wait(i) + spread * wn[q, k, :, cols].astype(F32)
            st[i] = state
            gather(i).wait_send()

            @pl.when(k != 3)
            def _():
                u[4 * h + i] = state.astype(BF16)

            @pl.when(k == 3)
            def _():
                message = mf[q].reshape(16, 16, 384).astype(F32)
                half = slice(8 * (i % 2), 8 * (i % 2) + 8)
                noise = message[:, half, :256].reshape(ROWS, 256)
                times = (message[:, :8, 256:] + message[:, 8:, 256:]).reshape(ROWS, 128)
                times = jnp.concatenate([times] * 2, axis=1)
                start = state.astype(BF16).astype(F32)
                end = xt[q, :, cols].astype(F32)
                mixed = (1.0 - times) * start + times * end + jnp.sqrt(times * (1.0 - times)) * NOISE_LEVEL * noise
                flow[i] = (end - mixed) / (1.0 - times)
                u[4 * h + i] = mixed.astype(BF16)

            gather(i).start()
        return clock - width

    lax.fori_loop(0, 4, step, jnp.float32(1.0))

    for i in (2, 3):
        load(i).wait()
        cross(i).wait()
    cross(9).start()
    message = mf[0].reshape(16, 16, 384)[:, :, 256:].astype(F32)
    times = (message[:, :8] + message[:, 8:]).reshape(ROWS, 128)
    times = jnp.concatenate([times] * 2, axis=1)

    def finish_fore(q, cols, product):
        hidden = product + times * fca[q, :, cols]
        acc[q, :, cols] = hidden
        ab[q, :, cols] = (hidden * jax.nn.sigmoid(hidden)).astype(BF16)

    factor = expand(fg_ref, fe, finish_fore)
    reduce_start(fr)
    act_ref[share] = ab[c]
    cross(10).start()
    for j in range(8):
        normh[j % 2, share, 256 * (j // 2) : 256 * (j // 2 + 1)] = (
            u[j].astype(F32) * factor * fg_ref[j]
        ).astype(BF16)
    cross(11).start()
    cross(9).wait()
    for i in range(2):
        walk_ref[share, 256 * i : 256 * (i + 1)] = st[2 * c + i]
        walk_ref[other, 256 * i : 256 * (i + 1)] = wx[i]
    scale = 1.0 / (8192.0**0.5)
    for i in range(4):
        j = 4 * h + i
        err[j, share] = ((reduce_wait(i) - flow[i]) * scale).astype(BF16)
        gather_err(i).start()
        cross_err(j, i).start()
    for i in range(4):
        gather(i).wait_send()
    cross(10).wait()
    cross(11).wait()

    def pair_normed():
        return remote(normh.at[1 - l, share], pn.at[share], gs.at[26], gr.at[26], pair_dev)

    def ydev(d):
        return device(z, l, (y + d) % 4, h, c)

    def zdev(d):
        return device((z + d) % 4, l, y, h, c)

    def pair_forward():
        return remote(pn.at[share], pn.at[share], gs.at[27], gr.at[27], core_dev)

    def pair_grad(s):
        part = share if s == 0 else other
        return remote(hg_ref.at[part], ph.at[part], gs.at[28 + s], gr.at[28 + s], pair_dev)

    def r_first_y(d):
        return remote(gy_r.at[:, :, (y + d) % 4], r1y_r.at[d - 1], gs.at[d - 1], gr.at[d - 1], ydev(d))

    def r_first_z(d):
        return remote(gz_r.at[(z + d) % 4], r1z_r.at[d - 1], gs.at[2 + d], gr.at[2 + d], zdev(d))

    def r_second_y(d):
        return remote(ay_r.at[(z + d) % 4], r2_r.at[0, d - 1], gs.at[5 + d], gr.at[5 + d], zdev(d))

    def r_second_z(d):
        return remote(az_r.at[:, (y + d) % 4], r2_r.at[1, d - 1], gs.at[8 + d], gr.at[8 + d], ydev(d))

    def r_third(i):
        return remote(s_r.at[i], r3_r.at[i], gs.at[12 + i], gr.at[12 + i], pair_dev)

    def e_first_y(d):
        return remote(gy_e.at[:, (y + d) % 4], r1y_e.at[d - 1], gs.at[13 + d], gr.at[13 + d], ydev(d))

    def e_first_z(d):
        return remote(gz_e.at[(z + d) % 4], r1z_e.at[d - 1], gs.at[16 + d], gr.at[16 + d], zdev(d))

    def e_second_y(d):
        return remote(ay_e.at[(z + d) % 4], r2_e.at[0, d - 1], gs.at[19 + d], gr.at[19 + d], zdev(d))

    def e_second_z(d):
        return remote(az_e.at[(y + d) % 4], r2_e.at[1, d - 1], gs.at[22 + d], gr.at[22 + d], ydev(d))

    def outer(left, right):
        return lax.dot_general(left, right, (((0,), (0,)), ((), ())), preferred_element_type=F32)

    def make_r(to):
        for i in range(2):
            part = outer(err[2 * to + i], act_ref[...]).astype(BF16)
            gy_r[to, i] = part[:, :512].reshape(4, 64, 512)
            gz_r[to, i] = part[:, 512:].reshape(4, 64, 512)
            for d in (1, 2, 3):
                dst = (y + d) % 4
                remote(
                    gy_r.at[to, i, dst], r1y_r.at[d - 1, to, i], gs.at[d - 1], gr.at[d - 1], ydev(d)
                ).start()
        for d in (1, 2, 3):

            @pl.when(to == (z + d) % 4)
            def _():
                r_first_z(d).start()

    for half in range(2):
        for i in range(2):
            cross_err(4 * h + 2 * half + i, 2 * half + i).wait_recv()
        make_r(2 * h + half)
    for i in range(4):
        gather_err(i).wait_recv()
        cross_err(4 * (1 - h) + i, 4 + i).start()
    pair_normed().start()
    for half in range(2):
        for i in range(2):
            cross_err(4 * (1 - h) + 2 * half + i, 4 + 2 * half + i).wait_recv()
        make_r(2 * (1 - h) + half)

    rows_err = jnp.concatenate([err[j, share] for j in range(8)], axis=1)
    for k in range(2):
        q = c if k == 0 else 1 - c
        for n in range(4):
            cols = slice(256 * n, 256 * (n + 1))
            back = lax.dot_general(
                rows_err, fr[q, cols, :], (((1,), (1,)), ((), ())), preferred_element_type=F32
            )
            hidden = acc[q, :, cols]
            sig = jax.nn.sigmoid(hidden)
            value = (back * (sig * (1.0 + hidden * (1.0 - sig)))).astype(BF16)
            if k == 0:
                hg_ref[share, cols] = value
            else:
                hs[:, cols] = value
        if k == 0:
            pair_grad(0).start()
        else:
            cross(12).start()
    cross(12).wait()
    pair_grad(1).start()
    for i in range(4):
        gather_err(i).wait_send()
        cross_err(4 * h + i, i).wait_send()
        cross_err(4 * (1 - h) + i, 4 + i).wait_send()

    pair_normed().wait()
    pair_forward().start()
    pair_forward().wait()
    for s in range(2):
        pair_grad(s).wait()

    def make_e(j, _):
        to = (z + 1 + j) % 4
        column = pl.ds(pl.multiple_of(to * 256, 256), 256)
        part = (outer(normh[l, :, column], hg_ref[...]) + outer(pn[:, column], ph[...])).astype(BF16)
        gy_e[to] = part[:, :512].reshape(4, 64, 512)
        gz_e[to] = part[:, 512:].reshape(4, 64, 512)
        for d in (1, 2, 3):
            dst = (y + d) % 4
            remote(
                gy_e.at[to, dst], r1y_e.at[d - 1, to], gs.at[13 + d], gr.at[13 + d], ydev(d)
            ).start()
        return 0

    for d in (1, 2, 3):
        lax.fori_loop(d - 1, d, make_e, 0)
        e_first_z(d).start()
    lax.fori_loop(3, 4, make_e, 0)

    for d in (1, 2, 3):
        r_first_y(d).wait()

    def add_ry(i, _):
        total = gy_r[i, :, y].astype(F32) + sum(r1y_r[d, i].astype(F32) for d in range(3))
        ay_r[i] = total.astype(BF16)
        return 0

    lax.fori_loop(0, 4, add_ry, 0)
    for d in (1, 2, 3):
        r_second_y(d).start()
    for d in (1, 2, 3):
        r_first_z(d).wait()

    def add_rz(i, _):
        total = gz_r[z, :, i].astype(F32) + sum(r1z_r[d, :, i].astype(F32) for d in range(3))
        az_r[:, i] = total.astype(BF16)
        return 0

    lax.fori_loop(0, 4, add_rz, 0)
    for d in (1, 2, 3):
        r_second_z(d).start()

    def finish_r(i):
        for d in (1, 2, 3):
            (r_second_y(d) if i == 0 else r_second_z(d)).wait()

        def own(side):
            return ay_r[z, side] if i == 0 else az_r[side, y]

        s_r[i] = (
            own(1 - l).astype(F32) + sum(r2_r[i, d, 1 - l].astype(F32) for d in range(3))
        ).astype(BF16)
        r_third(i).start()
        b_r[i] = own(l).astype(F32) + sum(r2_r[i, d, l].astype(F32) for d in range(3))

    finish_r(0)
    finish_r(1)

    for d in (1, 2, 3):
        e_first_y(d).wait()

    def add_ey(i, _):
        total = gy_e[i, y].astype(F32) + sum(r1y_e[d, i].astype(F32) for d in range(3))
        ay_e[i] = total.astype(BF16)
        return 0

    lax.fori_loop(0, 4, add_ey, 0)
    for d in (1, 2, 3):
        e_second_y(d).start()
    for d in (1, 2, 3):
        e_first_z(d).wait()

    def add_ez(i, _):
        total = gz_e[z, i].astype(F32) + sum(r1z_e[d, i].astype(F32) for d in range(3))
        az_e[i] = total.astype(BF16)
        return 0

    lax.fori_loop(0, 4, add_ez, 0)
    for d in (1, 2, 3):
        e_second_z(d).start()
    for i in range(2):
        r_third(i).wait()
        gr_ref[:, 512 * i : 512 * (i + 1)] = b_r[i] + r3_r[i].astype(F32)
    for i in range(2):
        for d in (1, 2, 3):
            (e_second_y(d) if i == 0 else e_second_z(d)).wait()
        mine = ay_e[z] if i == 0 else az_e[y]
        ge_ref[:, 512 * i : 512 * (i + 1)] = mine.astype(F32) + sum(r2_e[i, d].astype(F32) for d in range(3))


def copy_kernel(a_in, b_in, c_in, a_out, b_out, c_out, a_mid, b_mid, c_mid, sems):
    trios = ((a_in, a_mid, a_out), (b_in, b_mid, b_out), (c_in, c_mid, c_out))
    into = [pltpu.make_async_copy(src, mid, sems.at[0, i]) for i, (src, mid, dst) in enumerate(trios)]
    out = [pltpu.make_async_copy(mid, dst, sems.at[1, i]) for i, (src, mid, dst) in enumerate(trios)]
    for copy in into:
        copy.start()
    for first, second in zip(into, out):
        first.wait()
        second.start()
    for copy in out:
        copy.wait()


def body(
    target_latents, walk_noise, step_sizes, back_gain, back_expand, back_clock, back_reduce,
    bridge_times, bridge_noise, fore_gain, fore_expand, fore_clock, fore_reduce,
):
    vmem = pl.BlockSpec(memory_space=pltpu.VMEM)
    smem = pl.BlockSpec(memory_space=pltpu.SMEM)
    hbm = pl.BlockSpec(memory_space=pl.ANY)
    dma = pltpu.SemaphoreType.DMA
    sds = jax.ShapeDtypeStruct
    R = ROWS
    outs = pl.pallas_call(
        net_kernel,
        out_shape=(sds((256, 512), F32), sds((64, 1024), F32), sds((64, 1024), F32)),
        in_specs=[vmem, hbm, smem, vmem, hbm, vmem, hbm, vmem, vmem, vmem, hbm, vmem, hbm],
        out_specs=(vmem,) * 3,
        scratch_shapes=[
            pltpu.VMEM((2, 2048, 1024), BF16), pltpu.VMEM((2, 1024, 2048), BF16),
            pltpu.VMEM((2, 2048, 1024), BF16), pltpu.VMEM((2, 1024, 2048), BF16),
            pltpu.VMEM((2, 1, 1024), F32), pltpu.VMEM((2, 1, 1024), F32),
            pltpu.VMEM((2, 4, R, 512), BF16), pltpu.VMEM((2, R, 512), BF16),
            pltpu.VMEM((8, R, 256), BF16), pltpu.VMEM((4, R, 256), F32),
            pltpu.VMEM((2, R, 1024), F32), pltpu.VMEM((2, R, 1024), BF16),
            pltpu.VMEM((4, R, 256), F32), pltpu.VMEM((4, R, 256), BF16), pltpu.VMEM((4, R, 256), BF16),
            pltpu.VMEM((4, R, 256), F32),
        ]
        + [pltpu.VMEM((4, 2, 4, 16, 384), BF16)] * 4
        + [
            pltpu.VMEM((2, 2, 2, 4, 16, 384), BF16), pltpu.VMEM((2, R, 256), F32),
            pltpu.VMEM((8, 256, 256), BF16), pltpu.VMEM((2, 256, 1024), BF16),
            pltpu.VMEM((256, 1024), BF16), pltpu.VMEM((256, 1024), BF16), pltpu.VMEM((R, 1024), BF16),
            pltpu.VMEM((256, 1024), BF16), pltpu.VMEM((256, 1024), BF16),
            pltpu.VMEM((4, 2, 4, 64, 512), BF16), pltpu.VMEM((4, 2, 4, 64, 512), BF16),
            pltpu.VMEM((3, 4, 2, 64, 512), BF16), pltpu.VMEM((3, 2, 4, 64, 512), BF16),
            pltpu.VMEM((4, 2, 64, 512), BF16), pltpu.VMEM((2, 4, 64, 512), BF16),
            pltpu.VMEM((2, 3, 2, 64, 512), BF16),
            pltpu.VMEM((2, 64, 512), F32), pltpu.VMEM((2, 64, 512), BF16), pltpu.VMEM((2, 64, 512), BF16),
            pltpu.VMEM((4, 4, 64, 512), BF16), pltpu.VMEM((4, 4, 64, 512), BF16),
            pltpu.VMEM((3, 4, 64, 512), BF16), pltpu.VMEM((3, 4, 64, 512), BF16),
            pltpu.VMEM((4, 64, 512), BF16), pltpu.VMEM((4, 64, 512), BF16),
            pltpu.VMEM((2, 3, 64, 512), BF16),
        ]
        + [dma((5,)), dma((21,)), dma((21,)), dma((12,)), dma((12,)), dma((7,)), dma((7,)), dma((30,)), dma((30,))],
        compiler_params=pltpu.CompilerParams(
            collective_id=0, has_side_effects=True, vmem_limit_bytes=62 * 2**20
        ),
        name="net",
    )(
        target_latents, walk_noise, step_sizes, back_gain.reshape(8, 1, 256), back_expand,
        back_clock.reshape(1, 1024), back_reduce, bridge_times.reshape(2, 128), bridge_noise,
        fore_gain.reshape(8, 1, 256), fore_expand, fore_clock.reshape(1, 1024), fore_reduce,
    )
    return pl.pallas_call(
        copy_kernel,
        out_shape=tuple(sds(o.shape, o.dtype) for o in outs),
        in_specs=[hbm] * 3,
        out_specs=(hbm,) * 3,
        scratch_shapes=[pltpu.VMEM(o.shape, o.dtype) for o in outs] + [dma((2, 3))],
        name="place_outputs",
    )(*outs)


def solution(mesh):
    placed = (
        P("batch", "tensor"), P(None, "batch", "tensor"), P(), P(), P(None, "tensor"), P("tensor"),
        P("tensor", None), P("batch"), P("batch", "tensor"), P(), P(None, "tensor"), P("tensor"),
        P("tensor", None),
    )
    return jax.shard_map(
        body, mesh=mesh, in_specs=placed,
        out_specs=(P("batch", "tensor"), P("batch", "tensor"), P("batch", "tensor")), check_vma=False,
    )
```

time: 154 us -> 146 us (0.948)
  Pallas kernels: 153 us -> 145 us
    pallas_call x1, Pallas kernels: 151 us -> 143 us  [body(): pl.pallas_call(net_kernel, out_shape=(sds((256, 512), F32), sds((64, 1024...]
where the time goes in v3:
time: 146 us; the launch traced here: 145 us
  Pallas kernels  145 us (99%)
    pallas_call x1, Pallas kernels, body(): pl.pallas_call(net_kernel, out_shape=(sds((256, 512), F32), sds((64, 1024...  143 us

profile of v3, /device:TPU:0, one launch (start us, length us, event | category | flops | bytes accessed | tf_op | source)
XLA Modules:
  0.0 145.4 jit_solution(18075646434004558429)
XLA Ops:
  0.6 142.5 %net.1 = (f32[256,512]{1,0:T(8,128)}, f32[64,1024]{1,0:T(8,128)}, f32[64,1024]{1,0:T(8,128)}) custom-call(bf16[256,512]{1,0:T(8,128)(2,1)} %x_ref.1, bf16[4,256,512]{2,1,0:T(8,128)(2,1)} %wn_hbm.1, f32[4]{0:T(128)} %steps_ref.1, f32[8,1,256]{2,1,0:T(1,128)} %bitcast.5, bf16[2048,1024]{1,0:T(8,128)(2,1)} %be_hbm.1, f32[1,1024]{1,0:T(1,128)} %bitcast.7, ...), custom_call_target="tpu_custom_call" | custom-call | tf_op jit(solution)/shard_map/net/pallas_call | solution.py:534
  143.2 2.1 %place_outputs.1 = (f32[256,512]{1,0:T(8,128)}, f32[64,1024]{1,0:T(8,128)}, f32[64,1024]{1,0:T(8,128)}) custom-call(f32[256,512]{1,0:T(8,128)} %get-tuple-element.6.a_in, f32[64,1024]{1,0:T(8,128)} %get-tuple-element.7.b_in, f32[64,1024]{1,0:T(8,128)} %get-tuple-element.8.c_in), custom_call_target="tpu_custom_call" | custom-call | tf_op jit(solution)/shard_map/place_outputs/pallas_call | solution.py:575

commit v4 on v3

--- a/solution.py
+++ b/solution.py
@@ -11,6 +11,8 @@
 F32 = jnp.float32
 BF16 = jnp.bfloat16
 ROWS = 128
+WIDE = 640
+NARROW = 384
 
 
 def place():
@@ -48,7 +50,7 @@
     walk_ref, ge_ref, gr_ref,
     be, br, fe, fr, bca, fca, wn, xt, u, st, acc, ab, own, pfs, pfr, flow, m0, m1, m2, m3, mf, wx,
     err, normh, act_ref, hg_ref, hs, pn, ph,
-    gy_r, gz_r, r1y_r, r1z_r, ay_r, az_r, r2_r, b_r, s_r, r3_r,
+    gy_r, gz_r, r1y_r, r1z_r, ay_r, az_r, r2y_r, r2z_r, b_r, s_r, r3_r,
     gy_e, gz_e, r1y_e, r1z_e, ay_e, az_e, r2_e,
     load_sem, cs, cr, fs, fr_sem, ms, mr, gs, gr,
 ):
@@ -56,8 +58,12 @@
     core_dev = device(z, l, y, h, 1 - c)
     far_dev = device(z, l, y, 1 - h, c)
     pair_dev = device(z, 1 - l, y, h, c)
+    cut_dev = device(z, 1 - l, y, 1 - h, c)
     share = pl.ds(pl.multiple_of(c * 128, 128), 128)
     other = pl.ds(pl.multiple_of((1 - c) * 128, 128), 128)
+
+    near_cols = pl.ds(pl.multiple_of(h * 1024, 1024), 1024)
+    far_cols = pl.ds(pl.multiple_of((1 - h) * 1024, 1024), 1024)
 
     def load(i):
         src, dst = (
@@ -68,7 +74,8 @@
 
     def cross(i):
         src, dst = (
-            (be_hbm, be.at[c]), (br_hbm, br.at[c]), (fe_hbm, fe.at[c]), (fr_hbm, fr.at[c]),
+            (be_hbm, be.at[c]), (br_hbm.at[:, far_cols], br.at[c, :, far_cols]),
+            (fe_hbm, fe.at[c]), (fr_hbm, fr.at[c]),
             (wn_hbm.at[:, other], wn.at[c]),
             (x_ref.at[other], xt.at[c]),
             (bca.at[c], bca.at[c]), (fca.at[c], fca.at[c]),
@@ -77,11 +84,12 @@
             (ab.at[1 - c], act_ref.at[share]),
             (normh.at[:, share], normh.at[:, share]),
             (hs, hg_ref.at[share]),
+            (br_hbm.at[:, near_cols], br.at[c, :, near_cols]),
         )[i]
         return remote(src, dst, cs.at[i], cr.at[i], core_dev)
 
     def cross_err(j, i):
-        return remote(err.at[j, share], err.at[j, share], cs.at[13 + i], cr.at[13 + i], core_dev)
+        return remote(err.at[j, share], err.at[j, share], cs.at[14 + i], cr.at[14 + i], core_dev)
 
     def gather(i):
         return remote(u.at[4 * h + i], u.at[4 * h + i], fs.at[i], fr_sem.at[i], far_dev)
@@ -95,7 +103,7 @@
 
     for i in (0, 1, 4):
         load(i).start()
-    arrived = greet([core_dev, far_dev] + batch_peers(z, l, y, h, c))
+    arrived = greet([core_dev, far_dev, cut_dev] + batch_peers(z, l, y, h, c))
     bca[c] = bc_ref[...]
     fca[c] = fc_ref[...]
     for i in range(2):
@@ -113,6 +121,7 @@
         u[4 * h + 2 * (1 - c) + i] = xt[1 - c, :, 256 * i : 256 * (i + 1)]
         gather(2 * (1 - c) + i).start()
     cross(1).start()
+    cross(13).start()
     cross(4).start()
     for i in range(4):
         st[i] = u[4 * h + i].astype(F32)
@@ -183,10 +192,11 @@
             ab[1], weights[1, :, cols], preferred_element_type=F32
         )
 
-    def reduce_start(weights):
+    def reduce_start(weights, between=lambda: None):
         for i in range(4):
             pfs[i] = contract(weights, 4 * (1 - h) + i).astype(BF16)
             reduce(i).start()
+        between()
         for i in range(4):
             own[i] = contract(weights, 4 * h + i)
 
@@ -213,7 +223,12 @@
         def _():
             cross(1).wait()
 
-        reduce_start(br)
+        def rest():
+            @pl.when(k == 0)
+            def _():
+                cross(13).wait()
+
+        reduce_start(br, rest)
 
         @pl.when(k == 0)
         def _():
@@ -312,8 +327,10 @@
     cross(10).wait()
     cross(11).wait()
 
-    def pair_normed():
-        return remote(normh.at[1 - l, share], pn.at[share], gs.at[26], gr.at[26], pair_dev)
+    def pair_normed(i):
+        part = pl.ds(pl.multiple_of(c * 128 + 64 * i, 64), 64)
+        dev = pair_dev if i == 0 else cut_dev
+        return remote(normh.at[1 - l, part], pn.at[part], gs.at[26 + 4 * i], gr.at[26 + 4 * i], dev)
 
     def ydev(d):
         return device(z, l, (y + d) % 4, h, c)
@@ -335,13 +352,16 @@
         return remote(gz_r.at[(z + d) % 4], r1z_r.at[d - 1], gs.at[2 + d], gr.at[2 + d], zdev(d))
 
     def r_second_y(d):
-        return remote(ay_r.at[(z + d) % 4], r2_r.at[0, d - 1], gs.at[5 + d], gr.at[5 + d], zdev(d))
+        return remote(ay_r.at[(z + d) % 4], r2y_r.at[d - 1], gs.at[5 + d], gr.at[5 + d], zdev(d))
 
     def r_second_z(d):
-        return remote(az_r.at[:, (y + d) % 4], r2_r.at[1, d - 1], gs.at[8 + d], gr.at[8 + d], ydev(d))
+        return remote(az_r.at[:, (y + d) % 4], r2z_r.at[d - 1], gs.at[8 + d], gr.at[8 + d], ydev(d))
+
+    parts_r = (slice(0, WIDE), slice(WIDE, WIDE + NARROW))
 
     def r_third(i):
-        return remote(s_r.at[i], r3_r.at[i], gs.at[12 + i], gr.at[12 + i], pair_dev)
+        cols = parts_r[i]
+        return remote(s_r.at[:, cols], r3_r.at[:, cols], gs.at[12 + i], gr.at[12 + i], pair_dev)
 
     def e_first_y(d):
         return remote(gy_e.at[:, (y + d) % 4], r1y_e.at[d - 1], gs.at[13 + d], gr.at[13 + d], ydev(d))
@@ -361,8 +381,8 @@
     def make_r(to):
         for i in range(2):
             part = outer(err[2 * to + i], act_ref[...]).astype(BF16)
-            gy_r[to, i] = part[:, :512].reshape(4, 64, 512)
-            gz_r[to, i] = part[:, 512:].reshape(4, 64, 512)
+            gy_r[to, i] = part[:, :WIDE].reshape(4, 64, WIDE)
+            gz_r[to, i] = part[:, WIDE:].reshape(4, 64, NARROW)
             for d in (1, 2, 3):
                 dst = (y + d) % 4
                 remote(
@@ -374,6 +394,8 @@
             def _():
                 r_first_z(d).start()
 
+    for i in range(2):
+        pair_normed(i).start()
     for half in range(2):
         for i in range(2):
             cross_err(4 * h + 2 * half + i, 2 * half + i).wait_recv()
@@ -381,12 +403,6 @@
     for i in range(4):
         gather_err(i).wait_recv()
         cross_err(4 * (1 - h) + i, 4 + i).start()
-    pair_normed().start()
-    for half in range(2):
-        for i in range(2):
-            cross_err(4 * (1 - h) + 2 * half + i, 4 + 2 * half + i).wait_recv()
-        make_r(2 * (1 - h) + half)
-
     rows_err = jnp.concatenate([err[j, share] for j in range(8)], axis=1)
     for k in range(2):
         q = c if k == 0 else 1 - c
@@ -406,14 +422,20 @@
             pair_grad(0).start()
         else:
             cross(12).start()
-    cross(12).wait()
-    pair_grad(1).start()
+    for half in range(2):
+        for i in range(2):
+            cross_err(4 * (1 - h) + 2 * half + i, 4 + 2 * half + i).wait_recv()
+        make_r(2 * (1 - h) + half)
+        if half == 0:
+            cross(12).wait()
+            pair_grad(1).start()
     for i in range(4):
         gather_err(i).wait_send()
         cross_err(4 * h + i, i).wait_send()
         cross_err(4 * (1 - h) + i, 4 + i).wait_send()
 
-    pair_normed().wait()
+    pair_normed(0).wait()
+    pair_normed(1).wait()
     pair_forward().start()
     pair_forward().wait()
     for s in range(2):
@@ -467,11 +489,12 @@
         def own(side):
             return ay_r[z, side] if i == 0 else az_r[side, y]
 
-        s_r[i] = (
-            own(1 - l).astype(F32) + sum(r2_r[i, d, 1 - l].astype(F32) for d in range(3))
+        landed = r2y_r if i == 0 else r2z_r
+        s_r[:, parts_r[i]] = (
+            own(1 - l).astype(F32) + sum(landed[d, 1 - l].astype(F32) for d in range(3))
         ).astype(BF16)
         r_third(i).start()
-        b_r[i] = own(l).astype(F32) + sum(r2_r[i, d, l].astype(F32) for d in range(3))
+        b_r[:, parts_r[i]] = own(l).astype(F32) + sum(landed[d, l].astype(F32) for d in range(3))
 
     finish_r(0)
     finish_r(1)
@@ -500,7 +523,7 @@
         e_second_z(d).start()
     for i in range(2):
         r_third(i).wait()
-        gr_ref[:, 512 * i : 512 * (i + 1)] = b_r[i] + r3_r[i].astype(F32)
+        gr_ref[:, parts_r[i]] = b_r[:, parts_r[i]] + r3_r[:, parts_r[i]].astype(F32)
     for i in range(2):
         for d in (1, 2, 3):
             (e_second_y(d) if i == 0 else e_second_z(d)).wait()
@@ -552,17 +575,17 @@
             pltpu.VMEM((8, 256, 256), BF16), pltpu.VMEM((2, 256, 1024), BF16),
             pltpu.VMEM((256, 1024), BF16), pltpu.VMEM((256, 1024), BF16), pltpu.VMEM((R, 1024), BF16),
             pltpu.VMEM((256, 1024), BF16), pltpu.VMEM((256, 1024), BF16),
-            pltpu.VMEM((4, 2, 4, 64, 512), BF16), pltpu.VMEM((4, 2, 4, 64, 512), BF16),
-            pltpu.VMEM((3, 4, 2, 64, 512), BF16), pltpu.VMEM((3, 2, 4, 64, 512), BF16),
-            pltpu.VMEM((4, 2, 64, 512), BF16), pltpu.VMEM((2, 4, 64, 512), BF16),
-            pltpu.VMEM((2, 3, 2, 64, 512), BF16),
-            pltpu.VMEM((2, 64, 512), F32), pltpu.VMEM((2, 64, 512), BF16), pltpu.VMEM((2, 64, 512), BF16),
+            pltpu.VMEM((4, 2, 4, 64, WIDE), BF16), pltpu.VMEM((4, 2, 4, 64, NARROW), BF16),
+            pltpu.VMEM((3, 4, 2, 64, WIDE), BF16), pltpu.VMEM((3, 2, 4, 64, NARROW), BF16),
+            pltpu.VMEM((4, 2, 64, WIDE), BF16), pltpu.VMEM((2, 4, 64, NARROW), BF16),
+            pltpu.VMEM((3, 2, 64, WIDE), BF16), pltpu.VMEM((3, 2, 64, NARROW), BF16),
+            pltpu.VMEM((64, 1024), F32), pltpu.VMEM((64, 1024), BF16), pltpu.VMEM((64, 1024), BF16),
             pltpu.VMEM((4, 4, 64, 512), BF16), pltpu.VMEM((4, 4, 64, 512), BF16),
             pltpu.VMEM((3, 4, 64, 512), BF16), pltpu.VMEM((3, 4, 64, 512), BF16),
             pltpu.VMEM((4, 64, 512), BF16), pltpu.VMEM((4, 64, 512), BF16),
             pltpu.VMEM((2, 3, 64, 512), BF16),
         ]
-        + [dma((5,)), dma((21,)), dma((21,)), dma((12,)), dma((12,)), dma((7,)), dma((7,)), dma((30,)), dma((30,))],
+        + [dma((5,)), dma((22,)), dma((22,)), dma((12,)), dma((12,)), dma((7,)), dma((7,)), dma((31,)), dma((31,))],
         compiler_params=pltpu.CompilerParams(
             collective_id=0, has_side_effects=True, vmem_limit_bytes=62 * 2**20
         ),

time: 146 us -> 142 us (0.973)
  Pallas kernels: 145 us -> 141 us
    pallas_call x1, Pallas kernels: 143 us -> 139 us  [body(): pl.pallas_call(net_kernel, out_shape=(sds((256, 512), F32), sds((64, 1024...]
where the time goes in v4:
time: 142 us
  Pallas kernels  141 us (99%)
    pallas_call x1, Pallas kernels, body(): pl.pallas_call(net_kernel, out_shape=(sds((256, 512), F32), sds((64, 1024...  139 us

profile of v4, /device:TPU:0, one launch (start us, length us, event | category | flops | bytes accessed | tf_op | source)
XLA Modules:
  0.0 141.9 jit_solution(15768687833321317077)
XLA Ops:
  0.6 139.1 %net.1 = (f32[256,512]{1,0:T(8,128)}, f32[64,1024]{1,0:T(8,128)}, f32[64,1024]{1,0:T(8,128)}) custom-call(bf16[256,512]{1,0:T(8,128)(2,1)} %x_ref.1, bf16[4,256,512]{2,1,0:T(8,128)(2,1)} %wn_hbm.1, f32[4]{0:T(128)} %steps_ref.1, f32[8,1,256]{2,1,0:T(1,128)} %bitcast.5, bf16[2048,1024]{1,0:T(8,128)(2,1)} %be_hbm.1, f32[1,1024]{1,0:T(1,128)} %bitcast.7, ...), custom_call_target="tpu_custom_call" | custom-call | tf_op jit(solution)/shard_map/net/pallas_call | solution.py:557
  139.7 2.1 %place_outputs.1 = (f32[256,512]{1,0:T(8,128)}, f32[64,1024]{1,0:T(8,128)}, f32[64,1024]{1,0:T(8,128)}) custom-call(f32[256,512]{1,0:T(8,128)} %get-tuple-element.6.a_in, f32[64,1024]{1,0:T(8,128)} %get-tuple-element.7.b_in, f32[64,1024]{1,0:T(8,128)} %get-tuple-element.8.c_in), custom_call_target="tpu_custom_call" | custom-call | tf_op jit(solution)/shard_map/place_outputs/pallas_call | solution.py:598

commit v5 on v4

--- a/solution.py
+++ b/solution.py
@@ -403,6 +403,10 @@
     for i in range(4):
         gather_err(i).wait_recv()
         cross_err(4 * (1 - h) + i, 4 + i).start()
+    for half in range(2):
+        for i in range(2):
+            cross_err(4 * (1 - h) + 2 * half + i, 4 + 2 * half + i).wait_recv()
+        make_r(2 * (1 - h) + half)
     rows_err = jnp.concatenate([err[j, share] for j in range(8)], axis=1)
     for k in range(2):
         q = c if k == 0 else 1 - c
@@ -422,13 +426,8 @@
             pair_grad(0).start()
         else:
             cross(12).start()
-    for half in range(2):
-        for i in range(2):
-            cross_err(4 * (1 - h) + 2 * half + i, 4 + 2 * half + i).wait_recv()
-        make_r(2 * (1 - h) + half)
-        if half == 0:
-            cross(12).wait()
-            pair_grad(1).start()
+    cross(12).wait()
+    pair_grad(1).start()
     for i in range(4):
         gather_err(i).wait_send()
         cross_err(4 * h + i, i).wait_send()
@@ -496,9 +495,6 @@
         r_third(i).start()
         b_r[:, parts_r[i]] = own(l).astype(F32) + sum(landed[d, l].astype(F32) for d in range(3))
 
-    finish_r(0)
-    finish_r(1)
-
     for d in (1, 2, 3):
         e_first_y(d).wait()
 
@@ -521,14 +517,16 @@
     lax.fori_loop(0, 4, add_ez, 0)
     for d in (1, 2, 3):
         e_second_z(d).start()
-    for i in range(2):
-        r_third(i).wait()
-        gr_ref[:, parts_r[i]] = b_r[:, parts_r[i]] + r3_r[:, parts_r[i]].astype(F32)
+    finish_r(0)
+    finish_r(1)
     for i in range(2):
         for d in (1, 2, 3):
             (e_second_y(d) if i == 0 else e_second_z(d)).wait()
         mine = ay_e[z] if i == 0 else az_e[y]
         ge_ref[:, 512 * i : 512 * (i + 1)] = mine.astype(F32) + sum(r2_e[i, d].astype(F32) for d in range(3))
+    for i in range(2):
+        r_third(i).wait()
+        gr_ref[:, parts_r[i]] = b_r[:, parts_r[i]] + r3_r[:, parts_r[i]].astype(F32)
 
 
 def copy_kernel(a_in, b_in, c_in, a_out, b_out, c_out, a_mid, b_mid, c_mid, sems):

time: 142 us -> 139 us (0.979)
  Pallas kernels: 141 us -> 138 us
    pallas_call x1, Pallas kernels: 139 us -> 136 us  [body(): pl.pallas_call(net_kernel, out_shape=(sds((256, 512), F32), sds((64, 1024...]
where the time goes in v5:
time: 139 us
  Pallas kernels  138 us (99%)
    pallas_call x1, Pallas kernels, body(): pl.pallas_call(net_kernel, out_shape=(sds((256, 512), F32), sds((64, 1024...  136 us

profile of v5, /device:TPU:0, one launch (start us, length us, event | category | flops | bytes accessed | tf_op | source)
XLA Modules:
  0.0 138.6 jit_solution(14768080101240134007)
XLA Ops:
  0.6 135.7 %net.1 = (f32[256,512]{1,0:T(8,128)}, f32[64,1024]{1,0:T(8,128)}, f32[64,1024]{1,0:T(8,128)}) custom-call(bf16[256,512]{1,0:T(8,128)(2,1)} %x_ref.1, bf16[4,256,512]{2,1,0:T(8,128)(2,1)} %wn_hbm.1, f32[4]{0:T(128)} %steps_ref.1, f32[8,1,256]{2,1,0:T(1,128)} %bitcast.5, bf16[2048,1024]{1,0:T(8,128)(2,1)} %be_hbm.1, f32[1,1024]{1,0:T(1,128)} %bitcast.7, ...), custom_call_target="tpu_custom_call" | custom-call | tf_op jit(solution)/shard_map/net/pallas_call | solution.py:555
  136.4 2.1 %place_outputs.1 = (f32[256,512]{1,0:T(8,128)}, f32[64,1024]{1,0:T(8,128)}, f32[64,1024]{1,0:T(8,128)}) custom-call(f32[256,512]{1,0:T(8,128)} %get-tuple-element.6.a_in, f32[64,1024]{1,0:T(8,128)} %get-tuple-element.7.b_in, f32[64,1024]{1,0:T(8,128)} %get-tuple-element.8.c_in), custom_call_target="tpu_custom_call" | custom-call | tf_op jit(solution)/shard_map/place_outputs/pallas_call | solution.py:596

commit v6 on v5

--- a/solution.py
+++ b/solution.py
@@ -394,16 +394,17 @@
             def _():
                 r_first_z(d).start()
 
-    for i in range(2):
-        pair_normed(i).start()
     for half in range(2):
         for i in range(2):
             cross_err(4 * h + 2 * half + i, 2 * half + i).wait_recv()
         make_r(2 * h + half)
-    for i in range(4):
-        gather_err(i).wait_recv()
-        cross_err(4 * (1 - h) + i, 4 + i).start()
     for half in range(2):
+        for i in range(2):
+            gather_err(2 * half + i).wait_recv()
+            cross_err(4 * (1 - h) + 2 * half + i, 4 + 2 * half + i).start()
+        if half == 1:
+            for i in range(2):
+                pair_normed(i).start()
         for i in range(2):
             cross_err(4 * (1 - h) + 2 * half + i, 4 + 2 * half + i).wait_recv()
         make_r(2 * (1 - h) + half)

time: 139 us -> 139 us (level)
  no operation moved by 1% of the time
where the time goes in v6:
time: 139 us
  Pallas kernels  138 us (99%)
    pallas_call x1, Pallas kernels, body(): pl.pallas_call(net_kernel, out_shape=(sds((256, 512), F32), sds((64, 1024...  136 us

profile of v6, /device:TPU:0, one launch (start us, length us, event | category | flops | bytes accessed | tf_op | source)
XLA Modules:
  0.0 138.6 jit_solution(9419713608115969253)
XLA Ops:
  0.6 135.7 %net.1 = (f32[256,512]{1,0:T(8,128)}, f32[64,1024]{1,0:T(8,128)}, f32[64,1024]{1,0:T(8,128)}) custom-call(bf16[256,512]{1,0:T(8,128)(2,1)} %x_ref.1, bf16[4,256,512]{2,1,0:T(8,128)(2,1)} %wn_hbm.1, f32[4]{0:T(128)} %steps_ref.1, f32[8,1,256]{2,1,0:T(1,128)} %bitcast.5, bf16[2048,1024]{1,0:T(8,128)(2,1)} %be_hbm.1, f32[1,1024]{1,0:T(1,128)} %bitcast.7, ...), custom_call_target="tpu_custom_call" | custom-call | tf_op jit(solution)/shard_map/net/pallas_call | solution.py:556
  136.4 2.1 %place_outputs.1 = (f32[256,512]{1,0:T(8,128)}, f32[64,1024]{1,0:T(8,128)}, f32[64,1024]{1,0:T(8,128)}) custom-call(f32[256,512]{1,0:T(8,128)} %get-tuple-element.6.a_in, f32[64,1024]{1,0:T(8,128)} %get-tuple-element.7.b_in, f32[64,1024]{1,0:T(8,128)} %get-tuple-element.8.c_in), custom_call_target="tpu_custom_call" | custom-call | tf_op jit(solution)/shard_map/place_outputs/pallas_call | solution.py:597

commit v7 on v6

--- a/solution.py
+++ b/solution.py
@@ -532,8 +532,12 @@
 
 def copy_kernel(a_in, b_in, c_in, a_out, b_out, c_out, a_mid, b_mid, c_mid, sems):
     trios = ((a_in, a_mid, a_out), (b_in, b_mid, b_out), (c_in, c_mid, c_out))
-    into = [pltpu.make_async_copy(src, mid, sems.at[0, i]) for i, (src, mid, dst) in enumerate(trios)]
-    out = [pltpu.make_async_copy(mid, dst, sems.at[1, i]) for i, (src, mid, dst) in enumerate(trios)]
+    into, out = [], []
+    for src, mid, dst in trios:
+        for first in range(0, src.shape[0], 32):
+            part = pl.ds(first, 32)
+            into.append(pltpu.make_async_copy(src.at[part], mid.at[part], sems.at[0, len(into)]))
+            out.append(pltpu.make_async_copy(mid.at[part], dst.at[part], sems.at[1, len(out)]))
     for copy in into:
         copy.start()
     for first, second in zip(into, out):
@@ -599,7 +603,7 @@
         out_shape=tuple(sds(o.shape, o.dtype) for o in outs),
         in_specs=[hbm] * 3,
         out_specs=(hbm,) * 3,
-        scratch_shapes=[pltpu.VMEM(o.shape, o.dtype) for o in outs] + [dma((2, 3))],
+        scratch_shapes=[pltpu.VMEM(o.shape, o.dtype) for o in outs] + [dma((2, 12))],
         name="place_outputs",
     )(*outs)
 

time: 139 us -> 139 us (level)
  no operation moved by 1% of the time
where the time goes in v7:
time: 139 us
  Pallas kernels  138 us (99%)
    pallas_call x1, Pallas kernels, body(): pl.pallas_call(net_kernel, out_shape=(sds((256, 512), F32), sds((64, 1024...  136 us

profile of v7, /device:TPU:0, one launch (start us, length us, event | category | flops | bytes accessed | tf_op | source)
XLA Modules:
  0.0 138.7 jit_solution(517334984208282717)
XLA Ops:
  0.6 135.7 %net.1 = (f32[256,512]{1,0:T(8,128)}, f32[64,1024]{1,0:T(8,128)}, f32[64,1024]{1,0:T(8,128)}) custom-call(bf16[256,512]{1,0:T(8,128)(2,1)} %x_ref.1, bf16[4,256,512]{2,1,0:T(8,128)(2,1)} %wn_hbm.1, f32[4]{0:T(128)} %steps_ref.1, f32[8,1,256]{2,1,0:T(1,128)} %bitcast.5, bf16[2048,1024]{1,0:T(8,128)(2,1)} %be_hbm.1, f32[1,1024]{1,0:T(1,128)} %bitcast.7, ...), custom_call_target="tpu_custom_call" | custom-call | tf_op jit(solution)/shard_map/net/pallas_call | solution.py:560
  136.4 2.2 %place_outputs.1 = (f32[256,512]{1,0:T(8,128)}, f32[64,1024]{1,0:T(8,128)}, f32[64,1024]{1,0:T(8,128)}) custom-call(f32[256,512]{1,0:T(8,128)} %get-tuple-element.6.a_in, f32[64,1024]{1,0:T(8,128)} %get-tuple-element.7.b_in, f32[64,1024]{1,0:T(8,128)} %get-tuple-element.8.c_in), custom_call_target="tpu_custom_call" | custom-call | tf_op jit(solution)/shard_map/place_outputs/pallas_call | solution.py:601
